TPU v7x, 128 devices: a whole 4x4x4 slice. The times are simulated.
128 devices in a mesh: row: 16 (over y, x), col: 8 (over z, core).
Axes of the slice: x: 4, y: 4, z: 4, core: 2. Of those that a mesh axis runs over, the one named last changes fastest.
Arguments:
- object_field: float32 [2, 8192, 4096], P(None, 'row', 'col'), may hold values from -6 to 6
- probe: float32 [2, 256, 256], replicated, may hold values from -6 to 6
- amplitude: float32 [16, 8, 4, 256, 256], P('row', 'col'), may hold values from 0.1 to 3
- positions: int32 [16, 8, 4, 2], P('row', 'col'), may hold values from 0 to 511
- counts: int32 [16, 8], P('row', 'col'), may hold values from 1 to 4, as said below
Outputs:
- object_out: float32 [2, 8192, 4096], P(None, 'row', 'col')
- probe_out: float32 [2, 256, 256], replicated
Inputs may be any that keep to these rules, and one draw needn't show every extreme that they name: `counts`: every device has 1 to 4 live slots, its first ones; some device has 4 in every draw and about a quarter have 4, the rest at most half of it.
All inputs are finite; a program needn't handle non-finite values.
Results may differ from a plain program's by a relative error of at most 0.0003.
Values sent between devices are 32-bit elements; how exact they have to be, the bound alone decides.
No kernel may reach another device: no remote copies, remote signals or barrier semaphores. Data moves between devices by JAX's collectives and lax.ppermute only.
A program may use at most 128 MiB of HBM per device.

v0:
```python
import math

import jax
import jax.numpy as jnp
import numpy as np
from jax import lax
from jax.experimental import pallas as pl
from jax.experimental.pallas import tpu as pltpu
from jax.sharding import PartitionSpec as P

PASSES = 3
F = 256
TILE = 512
WIDE = TILE + F
HALF = F // 2
LANES = 128
FRAMES_LIMIT = 22
BESIDE = 6
STRIP = 32

amp_floor = 0.1
object_damping = 0.5
probe_damping = 1.0

VMEM = pl.BlockSpec(memory_space=pltpu.VMEM)
SMEM = pl.BlockSpec(memory_space=pltpu.SMEM)


def passed_along(block, axis, distance):
    size = lax.axis_size(axis)
    route = [((i - distance) % size, i) for i in range(size)]
    return lax.ppermute(block, axis, route)


def split(x):
    high = x.astype(jnp.bfloat16)
    low = (x - high.astype(jnp.float32)).astype(jnp.bfloat16)
    return high, low


def tables():
    k = np.arange(F)
    angles = (k[:, None] * k[None, :] % F) * (-2.0 * math.pi / F)
    re = np.cos(angles) / math.sqrt(F)
    im = np.sin(angles) / math.sqrt(F)
    left = np.block([[re, -im], [im, re]]).astype(np.float32)
    right = np.block([[re, im], [-im, re]]).astype(np.float32)

    def terms(m):
        high = m.astype(jnp.bfloat16)
        low = (m - high.astype(np.float32)).astype(jnp.bfloat16)
        return high, low

    lh, ll = terms(left)
    rh, rl = terms(right)
    return np.concatenate([lh, lh, ll], 1), np.concatenate([rh, rh, rl], 0)


def stacked(re, im):
    h, l = split(jnp.concatenate([re, im], 0))
    return jnp.concatenate([h, l, h], 0)


def abreast(y):
    h, l = split(jnp.concatenate([y[:F], y[F:]], 1))
    return jnp.concatenate([h, l, h], 1)


def transforms(fields, left, right):
    ys = [jnp.dot(left[...], stacked(re, im), preferred_element_type=jnp.float32) for re, im in fields]
    zs = [jnp.dot(abreast(y), right[...], preferred_element_type=jnp.float32) for y in ys]
    return [(z[:, :F], z[:, F:]) for z in zs]


def window(ref, lead, r, c):
    r0 = pl.multiple_of((r // 8) * 8, 8)
    c0 = pl.multiple_of((c // LANES) * LANES, LANES)
    rs, cs = r - r0, c - c0
    w = ref[lead + (pl.ds(r0, F + 8), pl.ds(c0, F + LANES))]
    lane = lax.broadcasted_iota(jnp.int32, (F + 8, LANES), 1)
    back = lax.rem(LANES - cs, LANES)
    t = [pltpu.roll(w[:, i * LANES : (i + 1) * LANES], back, 1) for i in range(3)]
    w = jnp.concatenate([jnp.where(lane < LANES - cs, t[i], t[i + 1]) for i in range(2)], 1)
    w = pltpu.roll(w.reshape(F // 8 + 1, 8, F), lax.rem(8 - rs, 8), 1)
    sub = lax.broadcasted_iota(jnp.int32, (F // 8, 8, F), 1)
    return jnp.where(sub < 8 - rs, w[:-1], w[1:]).reshape(F, F)


def deposit(ref, lead, r, c, x):
    r0 = pl.multiple_of((r // 8) * 8, 8)
    c0 = pl.multiple_of((c // LANES) * LANES, LANES)
    rs, cs = r - r0, c - c0
    w = pltpu.roll(x.reshape(F // 8, 8, F), rs, 1)
    zero = jnp.zeros((1, 8, F), jnp.float32)
    sub = lax.broadcasted_iota(jnp.int32, (F // 8 + 1, 8, F), 1)
    w = jnp.where(sub >= rs, jnp.concatenate([w, zero], 0), jnp.concatenate([zero, w], 0))
    w = w.reshape(F + 8, F)
    lane = lax.broadcasted_iota(jnp.int32, (F + 8, LANES), 1)
    a = pltpu.roll(w[:, :LANES], cs, 1)
    b = pltpu.roll(w[:, LANES:], cs, 1)
    t = [jnp.where(lane >= cs, a, 0.0), jnp.where(lane >= cs, b, a), jnp.where(lane >= cs, 0.0, b)]
    at = lead + (pl.ds(r0, F + 8), pl.ds(c0, F + LANES))
    ref[at] = ref[at] + jnp.concatenate(t, 1)


def visit_pair(i, mine, amplitude, left, right, ob, pr, canvas, grads):
    slots = (2 * i, 2 * i + 1)
    live = (1.0, (2 * i + 1 < mine[0, 8]).astype(jnp.float32))
    at = [(mine[0, k], mine[0, 4 + k]) for k in slots]
    patches = [[window(ob, (p,), r, c) for p in range(2)] for r, c in at]
    qr, qi = pr[0], pr[1]
    waves = [(qr * fr - qi * fi, qr * fi + qi * fr) for fr, fi in patches]
    turned = []
    for k, w, (zr, zi) in zip(slots, live, transforms(waves, left, right)):
        power = zr * zr + zi * zi
        ratio = (amplitude[k] * lax.rsqrt(jnp.maximum(power, amp_floor * amp_floor)) - 1.0) * w
        turned.append((zr * ratio, -(zi * ratio)))
    sums = [0.0, 0.0, 0.0]
    for w, (r, c), (fr, fi), (br, bi) in zip(live, at, patches, transforms(turned, left, right)):
        sums[0] = sums[0] + (fr * br - fi * bi)
        sums[1] = sums[1] - (fr * bi + fi * br)
        sums[2] = sums[2] + (fr * fr + fi * fi) * w
        deposit(canvas, (0,), r, c, qr * br - qi * bi)
        deposit(canvas, (1,), r, c, -(qr * bi) - qi * br)
    for p in range(3):
        grads[p] += sums[p]


def near_frames(infos, listed):
    total = jnp.int32(0)
    for a in range(3):
        for b in range(3):
            for k in range(4):
                r = infos[a][b, k] + (TILE * a - (TILE - F))
                c = infos[a][b, 4 + k] + (TILE * b - (TILE - F))
                use = (k < infos[a][b, 8]) & (r > 0) & (r < F + WIDE) & (c > 0) & (c < F + WIDE)
                listed[0, total] = r
                listed[1, total] = c
                total = total + use.astype(jnp.int32)
    return total


def visit_frames(mine, infos, amplitude, left, right, ob, pr, canvas, glow, grads, listed):
    n = near_frames(infos, listed)
    canvas[...] = jnp.zeros_like(canvas)
    glow[F : F + WIDE, F : F + WIDE] = jnp.zeros((WIDE, WIDE), jnp.float32)
    light = pr[0] * pr[0] + pr[1] * pr[1]

    def shine(i):
        used = (i < n).astype(jnp.float32)
        at = jnp.where(i < n, i, 0)
        deposit(glow, (), listed[0, at], listed[1, at], light * used)

    grads[...] = jnp.zeros_like(grads)

    def pair(i, carry):
        visit_pair(i, mine, amplitude, left, right, ob, pr, canvas, grads)
        for j in range(BESIDE):
            shine(i * BESIDE + j)
        return carry

    pairs = (mine[0, 8] + 1) // 2
    lax.fori_loop(0, pairs, pair, 0)

    def more(i, carry):
        shine(i)
        return carry

    lax.fori_loop(pairs * BESIDE, n, more, 0)


def hand_out(canvas, grads, zl_out, zr_out, up_out, mid_out, dn_out, g_out):
    zl_out[...] = canvas[:, :, :F]
    zr_out[...] = canvas[:, :, TILE:]
    up_out[:2] = canvas[:, :F, F:TILE]
    mid_out[...] = canvas[:, F:TILE, F:TILE]
    dn_out[:2] = canvas[:, TILE:, F:TILE]
    for p in range(3):
        for h in range(2):
            for t in range(2):
                g_out[pl.ds(4 * p + 2 * t + h, HALF, stride=12), :] = grads[p, h * HALF : (h + 1) * HALF, t * LANES : (t + 1) * LANES]


def start_kernel(tile, probe, ob, pr, own):
    ob[:, :TILE, :TILE] = tile[...]
    pr[...] = probe[...]
    me = lax.axis_index("row") * lax.axis_size("col") + lax.axis_index("col")
    picked = lax.broadcasted_iota(jnp.int32, (HALF, LANES), 0) == me
    rows = []
    for p in range(2):
        for t in range(2):
            for h in range(2):
                rows.append(jnp.sum(jnp.where(picked, probe[p, h * HALF : (h + 1) * HALF, t * LANES : (t + 1) * LANES], 0.0), axis=0, keepdims=True))
    own[...] = jnp.concatenate(rows, 0)


def first_kernel(mine, ia, ib, ic, amp, left, right, pr, tile, below, below_right, beside, corner, *rest):
    ob, light, outs, (unused, canvas, grads, listed, glow) = rest[0], rest[1], rest[2:8], rest[8:]
    ob[:, TILE:, :F] = below[...]
    ob[:, TILE:, F:TILE] = below_right[...]
    ob[:, :TILE, TILE:] = beside[...]
    ob[:, TILE:, TILE:] = corner[...]
    visit_frames(mine, (ia, ib, ic), amp, left, right, ob, pr, canvas, glow, grads, listed)
    light[...] = glow[F : F + WIDE, F : F + WIDE]
    hand_out(canvas, grads, *outs)


def gathered_probe(pg, pr):
    for p in range(2):
        for h in range(2):
            for t in range(2):
                pr[p, h * HALF : (h + 1) * HALF, t * LANES : (t + 1) * LANES] = pg[pl.ds(4 * p + 2 * t + h, HALF, stride=8), :]


def refreshed(put, size, o, l, zl, zr, up, mid, dn, left_in, right_in, cup, cdn, sup, sdn):
    for i in range(size // F):
        for j in range(size // F):
            for at in range(0, F, STRIP):
                here = slice(at, at + STRIP)
                rows, cols = slice(i * F + at, i * F + at + STRIP), slice(j * F, (j + 1) * F)
                scale = 1.0 / (l[rows, cols] + object_damping)
                for p in range(2):
                    if j == 0:
                        s = zl[p, rows, :] + left_in[p, rows, :]
                    elif j == 1:
                        s = (up, mid, dn)[i][p, here, :]
                    else:
                        s = zr[p, rows, :] + right_in[p, rows, :]
                    if i == 0:
                        s = s + (cdn[p, here, :] if j == 1 else sdn[j // 2, p, here, :])
                    if i == 2:
                        s = s + (cup[p, here, :] if j == 1 else sup[j // 2, p, here, :])
                    put(p, rows, cols, o[p, rows, cols] + s * scale)


def next_kernel(mine, ia, ib, ic, amp, left, right, pg, o, l, zl, zr, up, mid, dn, left_in, right_in, cup, cdn, sup, sdn, *rest):
    ob, light, outs, (pr, canvas, grads, listed, glow) = rest[0], rest[1], rest[2:8], rest[8:]

    def put(p, rows, cols, value):
        ob[p, rows, cols] = value

    refreshed(put, WIDE, o, l, zl, zr, up, mid, dn, left_in, right_in, cup, cdn, sup, sdn)
    gathered_probe(pg, pr)
    visit_frames(mine, (ia, ib, ic), amp, left, right, ob, pr, canvas, glow, grads, listed)
    light[...] = glow[F : F + WIDE, F : F + WIDE]
    hand_out(canvas, grads, *outs)


def last_kernel(pg, o, l, zl, up, mid, left_in, cdn, sdn, o_out, p_out):
    def put(p, rows, cols, value):
        o_out[p, rows, cols] = value

    refreshed(put, TILE, o, l, zl, None, up, mid, None, left_in, None, None, cdn, None, sdn)
    gathered_probe(pg, p_out)


def middle_kernel(last, g, old, zl, left_in, *rest):
    if last:
        sdn, new, spread = rest
        sdn[0] = zl[:, TILE:] + left_in[:, TILE:]
    else:
        zr, right_in, sup, sdn, new, spread = rest
        sup[0] = zl[:, :F] + left_in[:, :F]
        sup[1] = zr[:, :F] + right_in[:, :F]
        sdn[0] = zl[:, TILE:] + left_in[:, TILE:]
        sdn[1] = zr[:, TILE:] + right_in[:, TILE:]
    s = jnp.sum(g[...].reshape(HALF // 2, 24, LANES), axis=0)
    s = s[:12] + s[12:]
    value = old[...] + s[:8] / (jnp.concatenate([s[8:], s[8:]], 0) + probe_damping)
    new[...] = value
    spread[...] = jnp.broadcast_to(value[None], (HALF, 8, LANES)).reshape(HALF * 8, LANES)


def f32(*shape):
    return jax.ShapeDtypeStruct(shape, jnp.float32)


def call(kernel, args, outs, scratch=(), limit=14, smem=(), cost=None, alias=None):
    return pl.pallas_call(
        kernel,
        out_shape=tuple(outs),
        in_specs=[SMEM if i in smem else VMEM for i in range(len(args))],
        out_specs=tuple(VMEM for _ in outs),
        scratch_shapes=list(scratch),
        compiler_params=pltpu.CompilerParams(vmem_limit_bytes=limit << 20),
        cost_estimate=cost,
        input_output_aliases=alias or {},
    )(*args)


def call_frames(kernel, *args, alias=None):
    scratch = [
        pltpu.VMEM((2, F, F), jnp.float32),
        pltpu.VMEM((2, WIDE, WIDE), jnp.float32),
        pltpu.VMEM((3, F, F), jnp.float32),
        pltpu.SMEM((2, 40), jnp.int32),
        pltpu.VMEM((WIDE + 2 * F, WIDE + 2 * F), jnp.float32),
    ]
    outs = (
        f32(2, WIDE, WIDE), f32(WIDE, WIDE), f32(2, WIDE, F), f32(2, WIDE, F),
        f32(3, F, F), f32(2, F, F), f32(3, F, F), f32(HALF * 12, LANES),
    )
    return call(kernel, args, outs, scratch, limit=FRAMES_LIMIT, smem=(0, 1, 2, 3), alias=alias)


def everyone(x):
    return lax.all_to_all(x, ("row", "col"), 0, 0)


def shards(object_field, probe, amplitude, positions, counts):
    left, right = (jnp.asarray(t) for t in tables())
    amp = amplitude[0, 0]
    mine = jnp.concatenate([positions[0, 0, :, 0], positions[0, 0, :, 1], counts[0], jnp.zeros((7,), jnp.int32)])[None]

    below = passed_along(object_field[:, :F, :F], "row", -1)
    beside = passed_along(object_field[:, :, :F], "col", -1)
    below_right = passed_along(object_field[:, :F, F:], "row", -1)
    info = jnp.concatenate([passed_along(mine, "col", 1), mine, passed_along(mine, "col", -1)], 0)
    below, info = lax.optimization_barrier((below, info))
    infos = (passed_along(info, "row", 1), info, passed_along(info, "row", -1))
    corner = passed_along(below, "col", -1)
    wide, probe, own = call(start_kernel, (object_field, probe), (f32(2, WIDE, WIDE), f32(2, F, F), f32(8, LANES)))

    state = call_frames(
        first_kernel, mine, *infos, amp, left, right, probe, wide, below, below_right, beside, corner, alias={8: 0},
    )
    for sweep in range(PASSES):
        last = sweep == PASSES - 1
        ob, light, to_left, to_right, up, mid, down, grad = state
        grad = grad.reshape(HALF, 3, 4, LANES)
        from_left = passed_along(to_right, "col", 1)
        centre_down = passed_along(down, "row", 1)
        moved = [from_left, centre_down]
        if not last:
            moved += [passed_along(to_left, "col", -1), passed_along(up, "row", -1)]
        grad, to_left, to_right = lax.optimization_barrier((grad, to_left, to_right))
        grad = everyone(grad)
        grad, moved = lax.optimization_barrier((grad, moved))
        grad = grad.reshape(HALF * 12, LANES)
        tail = (f32(8, LANES), f32(HALF * 8, LANES))
        if last:
            from_left, centre_down = moved
            side_down, own, spread = call(
                lambda *refs: middle_kernel(True, *refs), (grad, own, to_left, from_left), (f32(1, 2, F, F),) + tail,
            )
            sides = (side_down,)
            moved = (passed_along(side_down, "row", 1),)
        else:
            from_left, centre_down, from_right, centre_up = moved
            side_up, side_down, own, spread = call(
                lambda *refs: middle_kernel(False, *refs), (grad, own, to_left, from_left, to_right, from_right),
                (f32(2, 2, F, F), f32(2, 2, F, F)) + tail,
            )
            sides = (side_up, side_down)
            moved = (passed_along(side_up, "row", -1), passed_along(side_down, "row", 1))
        sides, spread = lax.optimization_barrier((sides, spread))
        pg = everyone(spread.reshape(HALF, 2, 4, LANES)).reshape(HALF * 8, LANES)
        if last:
            return call(
                last_kernel, (pg, ob, light, to_left, up, mid, from_left, centre_down, moved[0]),
                (f32(2, TILE, TILE), f32(2, F, F)),
            )
        state = call_frames(
            next_kernel, mine, *infos, amp, left, right, pg, ob, light, to_left, to_right, up, mid, down,
            from_left, from_right, centre_up, centre_down, moved[0], moved[1], alias={8: 0},
        )


def solution(mesh):
    return jax.shard_map(
        shards,
        mesh=mesh,
        in_specs=(
            P(None, "row", "col"),
            P(),
            P("row", "col", None, None, None),
            P("row", "col", None, None),
            P("row", "col"),
        ),
        out_specs=(P(None, "row", "col"), P()),
        check_vma=False,
    )
```

profile of v0, /device:TPU:1, one launch (start us, length us, event | category | flops | bytes accessed | tf_op | source)
XLA Modules:
  0.0 272.0 jit_solution(6667528989876838786)
XLA Ops:
  0.6 1.4 fusion
  2.1 0.0 copy-start.5
  2.1 0.0 copy-start.4
  2.1 5.8 %collective-permute-start = (f32[2,256,256]{2,1,0:T(8,128)S(1)}, f32[2,256,256]{2,1,0:T(8,128)S(1)}, u32[]{:S(2)}, u32[]{:S(2)}) collective-permute-start(f32[2,256,256]{2,1,0:T(8,128)S(1)} %get-tuple-element.129), channel_id=1, source_target_pairs={{8,0},{16,8},{24,16},{32,24},{40,32},{48,40},{56,48},{64,56},{72,6... | collective-permute-start | bytes 1572872 | tf_op jit(solution)/shard_map/ppermute | solution.py:32
  7.9 0.1 slice.19
  8.1 0.0 copy-start
  8.1 0.0 copy-start.2
  8.1 1.0 collective-permute-start.6
  9.9 0.1 add_bitcast_fusion.mine
  10.0 3.0 %collective-permute-start.2 = (s32[1,16]{1,0:T(1,128)S(1)}, s32[1,16]{1,0:T(1,128)S(1)}, u32[]{:S(2)}, u32[]{:S(2)}) collective-permute-start(s32[1,16]{1,0:T(1,128)S(1)} %add_bitcast_fusion.mine), channel_id=1, source_target_pairs={{1,0},{2,1},{3,2},{4,3},{5,4},{6,5},{7,6},{0,7},{9,8},{10,9},{11,1... | collective-permute-start | bytes 200 | tf_op jit(solution)/shard_map/ppermute | solution.py:32
  13.0 0.5 collective-permute-start.5
  13.6 9.8 %collective-permute-done.2 = s32[1,16]{1,0:T(1,128)S(1)} collective-permute-done((s32[1,16]{1,0:T(1,128)S(1)}, s32[1,16]{1,0:T(1,128)S(1)}, u32[]{:S(2)}, u32[]{:S(2)}) %collective-permute-start.2) | collective-permute-done | bytes 96 | tf_op jit(solution)/shard_map/ppermute | solution.py:32
  23.4 1.3 collective-permute-start.7
  24.6 2.1 collective-permute-start.4
  26.8 0.0 collective-permute-start.3
  26.8 0.2 shard_map.86
  27.0 2.8 %collective-permute-done.5.below_right = f32[2,256,256]{2,1,0:T(8,128)S(1)} collective-permute-done((f32[2,256,256]{2,1,0:T(8,128)S(1)}, f32[2,256,256]{2,1,0:T(8,128)S(1)}, u32[]{:S(2)}, u32[]{:S(2)}) %collective-permute-start.5) | collective-permute-done | bytes 524320 | tf_op jit(solution)/shard_map/ppermute | solution.py:32
  29.8 0.0 collective-permute-done.4.ic
  29.8 2.7 collective-permute-done.3.ia
  32.5 0.0 collective-permute-done.7.corner
  32.5 0.0 collective-permute-done.6.beside
  32.5 6.8 %shard_map.87 = (f32[2,768,768]{2,1,0:T(8,128)S(1)}, f32[768,768]{1,0:T(8,128)S(1)}, f32[2,768,256]{2,1,0:T(8,128)S(1)}, f32[2,768,256]{2,1,0:T(8,128)S(1)}, f32...) custom-call(s32[1,16]{1,0:T(1,128)S(1)} %add_bitcast_fusion.mine, ...), custom_call_target="tpu_custom_call", output_to_operand_aliasing={{0}: (8, {})} | custom-call | tf_op jit(solution)/shard_map/pallas_call | solution.py:279
  39.3 3.4 %collective-permute-start.10 = (f32[2,768,256]{2,1,0:T(8,128)S(1)}, f32[2,768,256]{2,1,0:T(8,128)S(1)}, u32[]{:S(2)}, u32[]{:S(2)}) collective-permute-start(f32[2,768,256]{2,1,0:T(8,128)S(1)} %get-tuple-element.77.refs_2_.zl), channel_id=1, source_target_pairs={{1,0},{2,1},{3,2},{4,3},{5,4},{6,5},{7,6},{0,7},{9,8},{10,9},{11,1... | collective-permute-start | bytes 4718600 | tf_op jit(solution)/shard_map/ppermute | solution.py:32
  42.8 0.0 collective-permute-start.8
  42.8 0.0 collective-permute-start.9
  42.8 5.5 %collective-permute-start.11 = (f32[3,256,256]{2,1,0:T(8,128)S(1)}, f32[3,256,256]{2,1,0:T(8,128)S(1)}, u32[]{:S(2)}, u32[]{:S(2)}) collective-permute-start(f32[3,256,256]{2,1,0:T(8,128)S(1)} %get-tuple-element.74.up), channel_id=1, source_target_pairs={{8,0},{16,8},{24,16},{32,24},{40,32},{48,40},{56,48},{64,56},{72,6... | collective-permute-start | bytes 2359304 | tf_op jit(solution)/shard_map/ppermute | solution.py:32
  48.3 30.5 %all_to_all.30 = f32[128,3,4,128]{3,2,1,0:T(4,128)S(1)} all-to-all(f32[128,3,4,128]{3,2,1,0:T(4,128)S(1)} %bitcast.32), channel_id=1, replica_groups=mesh['row'=16,'col'=8] {'row','col'}, dimensions={0} | all-to-all | bytes 1572864 | tf_op jit(solution)/shard_map/all_to_all | solution.py:307
  78.8 0.0 collective-permute-done.9.cdn
  78.8 0.0 collective-permute-done.11.cup
  78.8 0.0 collective-permute-done.10.refs_5_.right_in
  78.8 0.3 shard_map.88
  79.2 2.3 collective-permute-start.12
  81.5 0.0 collective-permute-start.13
  81.5 35.4 %all_to_all.31 = f32[128,2,4,128]{3,2,1,0:T(4,128)S(1)} all-to-all(f32[128,2,4,128]{3,2,1,0:T(4,128)S(1)} %bitcast.33), channel_id=1, replica_groups=mesh['row'=16,'col'=8] {'row','col'}, dimensions={0} | all-to-all | bytes 1048576 | tf_op jit(solution)/shard_map/all_to_all | solution.py:307
  116.9 8.0 %shard_map.89 = (f32[2,768,768]{2,1,0:T(8,128)S(1)}, f32[768,768]{1,0:T(8,128)S(1)}, f32[2,768,256]{2,1,0:T(8,128)S(1)}, f32[2,768,256]{2,1,0:T(8,128)S(1)}, f32...) custom-call(s32[1,16]{1,0:T(1,128)S(1)} %add_bitcast_fusion.mine, ...), custom_call_target="tpu_custom_call", output_to_operand_aliasing={{0}: (8, {})} | custom-call | tf_op jit(solution)/shard_map/pallas_call | solution.py:279
  124.9 0.9 collective-permute-start.16
  125.8 0.8 collective-permute-start.14
  126.6 4.8 %collective-permute-start.17 = (f32[3,256,256]{2,1,0:T(8,128)S(1)}, f32[3,256,256]{2,1,0:T(8,128)S(1)}, u32[]{:S(2)}, u32[]{:S(2)}) collective-permute-start(f32[3,256,256]{2,1,0:T(8,128)S(1)} %get-tuple-element.95.up), channel_id=1, source_target_pairs={{8,0},{16,8},{24,16},{32,24},{40,32},{48,40},{56,48},{64,56},{72,6... | collective-permute-start | bytes 2359304 | tf_op jit(solution)/shard_map/ppermute | solution.py:32
  131.4 29.4 %all_to_all.32 = f32[128,3,4,128]{3,2,1,0:T(4,128)S(1)} all-to-all(f32[128,3,4,128]{3,2,1,0:T(4,128)S(1)} %bitcast.30), channel_id=1, replica_groups=mesh['row'=16,'col'=8] {'row','col'}, dimensions={0} | all-to-all | bytes 1572864 | tf_op jit(solution)/shard_map/all_to_all | solution.py:307
  160.8 0.4 shard_map.90
  161.2 4.4 %collective-permute-start.18 = (f32[2,2,256,256]{3,2,1,0:T(8,128)S(1)}, f32[2,2,256,256]{3,2,1,0:T(8,128)S(1)}, u32[]{:S(2)}, u32[]{:S(2)}) collective-permute-start(f32[2,2,256,256]{3,2,1,0:T(8,128)S(1)} %get-tuple-element.102), channel_id=1, source_target_pairs={{8,0},{16,8},{24,16},{32,24},{40,32},{48,40},{56,48},{64,56},{72,6... | collective-permute-start | bytes 3145736 | tf_op jit(solution)/shard_map/ppermute | solution.py:32
  165.6 35.0 %all_to_all.33 = f32[128,2,4,128]{3,2,1,0:T(4,128)S(1)} all-to-all(f32[128,2,4,128]{3,2,1,0:T(4,128)S(1)} %bitcast.34), channel_id=1, replica_groups=mesh['row'=16,'col'=8] {'row','col'}, dimensions={0} | all-to-all | bytes 1048576 | tf_op jit(solution)/shard_map/all_to_all | solution.py:307
  200.7 8.3 %shard_map.91 = (f32[2,768,768]{2,1,0:T(8,128)S(1)}, f32[768,768]{1,0:T(8,128)S(1)}, f32[2,768,256]{2,1,0:T(8,128)S(1)}, f32[2,768,256]{2,1,0:T(8,128)S(1)}, f32...) custom-call(s32[1,16]{1,0:T(1,128)S(1)} %add_bitcast_fusion.mine, ...), custom_call_target="tpu_custom_call", output_to_operand_aliasing={{0}: (8, {})} | custom-call | tf_op jit(solution)/shard_map/pallas_call | solution.py:279
  208.9 0.7 collective-permute-start.20
  209.7 33.6 %all_to_all.34 = f32[128,3,4,128]{3,2,1,0:T(4,128)S(1)} all-to-all(f32[128,3,4,128]{3,2,1,0:T(4,128)S(1)} %bitcast.31), channel_id=1, replica_groups=mesh['row'=16,'col'=8] {'row','col'}, dimensions={0} | all-to-all | bytes 1572864 | tf_op jit(solution)/shard_map/all_to_all | solution.py:307
  243.3 0.7 shard_map.92
  244.0 25.9 %all_to_all.35 = f32[128,2,4,128]{3,2,1,0:T(4,128)S(1)} all-to-all(f32[128,2,4,128]{3,2,1,0:T(4,128)S(1)} %bitcast.35), channel_id=1, replica_groups=mesh['row'=16,'col'=8] {'row','col'}, dimensions={0} | all-to-all | bytes 1048576 | tf_op jit(solution)/shard_map/all_to_all | solution.py:307
  270.0 2.0 shard_map.93
  (30 shorter events, 0.1 us)
Async XLA Ops:
  0.6 7.3 %copy-start.3 = (f32[2,512,512]{2,1,0:T(8,128)S(1)}, f32[2,512,512]{2,1,0:T(8,128)}, u32[]{:S(2)}) copy-start(f32[2,512,512]{2,1,0:T(8,128)} %tile.1) | copy-start | bytes 6291460
  2.1 7.8 %copy-start.5 = (s32[1,1,4,2]{2,3,1,0:T(2,128)S(1)}, s32[1,1,4,2]{2,3,1,0:T(2,128)}, u32[]{:S(2)}) copy-start(s32[1,1,4,2]{2,3,1,0:T(2,128)} %param.10) | copy-start | bytes 100
  2.1 24.7 %copy-start.4 = (f32[2,256,256]{2,1,0:T(8,128)S(1)}, f32[2,256,256]{2,1,0:T(8,128)}, u32[]{:S(2)}) copy-start(f32[2,256,256]{2,1,0:T(8,128)} %probe.1) | copy-start | bytes 1572868
  2.1 21.3 %collective-permute-start = (f32[2,256,256]{2,1,0:T(8,128)S(1)}, f32[2,256,256]{2,1,0:T(8,128)S(1)}, u32[]{:S(2)}, u32[]{:S(2)}) collective-permute-start(f32[2,256,256]{2,1,0:T(8,128)S(1)} %get-tuple-element.129), channel_id=1, source_target_pairs={{8,0},{16,8},{24,16},{32,24},{40,32},{48,40},{56,48},{64,56},{72,6... | collective-permute-start | bytes 1572872 | tf_op jit(solution)/shard_map/ppermute | solution.py:32
  7.9 24.6 %copy-start.1 = (bf16[512,1536]{1,0:T(8,128)(2,1)S(1)}, bf16[512,1536]{1,0:T(8,128)(2,1)}, u32[]{:S(2)}) copy-start(bf16[512,1536]{1,0:T(8,128)(2,1)} %constant.6.clone.left) | copy-start | bytes 4718596
  8.1 24.5 %copy-start = (bf16[1536,512]{1,0:T(8,128)(2,1)S(1)}, bf16[1536,512]{1,0:T(8,128)(2,1)}, u32[]{:S(2)}) copy-start(bf16[1536,512]{1,0:T(8,128)(2,1)} %constant.7.clone.right) | copy-start | bytes 4718596
  8.1 24.5 %copy-start.2 = (f32[1,1,4,256,256]{4,3,2,1,0:T(8,128)S(1)}, f32[1,1,4,256,256]{4,3,2,1,0:T(8,128)}, u32[]{:S(2)}) copy-start(f32[1,1,4,256,256]{4,3,2,1,0:T(8,128)} %param.9) | copy-start | bytes 3145732
  8.1 24.4 %collective-permute-start.6 = (f32[2,512,256]{2,1,0:T(8,128)S(1)}, f32[2,512,256]{2,1,0:T(8,128)S(1)}, u32[]{:S(2)}, u32[]{:S(2)}) collective-permute-start(f32[2,512,256]{2,1,0:T(8,128)S(1)} %slice.19), channel_id=1, source_target_pairs={{1,0},{2,1},{3,2},{4,3},{5,4},{6,5},{7,6},{0,7},{9,8},{10,9},{11,1... | collective-permute-start | bytes 3145736 | tf_op jit(solution)/shard_map/ppermute | solution.py:32
  10.0 13.4 %collective-permute-start.2 = (s32[1,16]{1,0:T(1,128)S(1)}, s32[1,16]{1,0:T(1,128)S(1)}, u32[]{:S(2)}, u32[]{:S(2)}) collective-permute-start(s32[1,16]{1,0:T(1,128)S(1)} %add_bitcast_fusion.mine), channel_id=1, source_target_pairs={{1,0},{2,1},{3,2},{4,3},{5,4},{6,5},{7,6},{0,7},{9,8},{10,9},{11,1... | collective-permute-start | bytes 200 | tf_op jit(solution)/shard_map/ppermute | solution.py:32
  13.0 10.3 %collective-permute-start.1 = (s32[1,16]{1,0:T(1,128)S(1)}, s32[1,16]{1,0:T(1,128)S(1)}, u32[]{:S(2)}, u32[]{:S(2)}) collective-permute-start(s32[1,16]{1,0:T(1,128)S(1)} %add_bitcast_fusion.mine), channel_id=1, source_target_pairs={{7,0},{0,1},{1,2},{2,3},{3,4},{4,5},{5,6},{6,7},{15,8},{8,9},{9,10... | collective-permute-start | bytes 200 | tf_op jit(solution)/shard_map/ppermute | solution.py:32
  13.0 16.8 %collective-permute-start.5 = (f32[2,256,256]{2,1,0:T(8,128)S(1)}, f32[2,256,256]{2,1,0:T(8,128)S(1)}, u32[]{:S(2)}, u32[]{:S(2)}) collective-permute-start(f32[2,256,256]{2,1,0:T(8,128)S(1)} %get-tuple-element.128), channel_id=1, source_target_pairs={{8,0},{16,8},{24,16},{32,24},{40,32},{48,40},{56,48},{64,56},{72,6... | collective-permute-start | bytes 1572872 | tf_op jit(solution)/shard_map/ppermute | solution.py:32
  23.4 9.1 %collective-permute-start.7 = (f32[2,256,256]{2,1,0:T(8,128)S(1)}, f32[2,256,256]{2,1,0:T(8,128)S(1)}, u32[]{:S(2)}, u32[]{:S(2)}) collective-permute-start(f32[2,256,256]{2,1,0:T(8,128)S(1)} %collective-permute-done.below), channel_id=1, source_target_pairs={{1,0},{2,1},{3,2},{4,3},{5,4},{6,5},{7,6},{0,7},{9,8},{10,9},{11,1... | collective-permute-start | bytes 1572872 | tf_op jit(solution)/shard_map/ppermute | solution.py:32
  24.6 5.2 %collective-permute-start.4 = (s32[3,16]{1,0:T(4,128)S(1)}, s32[3,16]{1,0:T(4,128)S(1)}, u32[]{:S(2)}, u32[]{:S(2)}) collective-permute-start(s32[3,16]{1,0:T(4,128)S(1)} %pad_add_fusion.ib), channel_id=1, source_target_pairs={{8,0},{16,8},{24,16},{32,24},{40,32},{48,40},{56,48},{64,56},{72,6... | collective-permute-start | bytes 584 | tf_op jit(solution)/shard_map/ppermute | solution.py:32
  26.8 5.8 %collective-permute-start.3 = (s32[3,16]{1,0:T(4,128)S(1)}, s32[3,16]{1,0:T(4,128)S(1)}, u32[]{:S(2)}, u32[]{:S(2)}) collective-permute-start(s32[3,16]{1,0:T(4,128)S(1)} %pad_add_fusion.ib), channel_id=1, source_target_pairs={{120,0},{0,8},{8,16},{16,24},{24,32},{32,40},{40,48},{48,56},{56,6... | collective-permute-start | bytes 584 | tf_op jit(solution)/shard_map/ppermute | solution.py:32
  39.3 39.5 %collective-permute-start.10 = (f32[2,768,256]{2,1,0:T(8,128)S(1)}, f32[2,768,256]{2,1,0:T(8,128)S(1)}, u32[]{:S(2)}, u32[]{:S(2)}) collective-permute-start(f32[2,768,256]{2,1,0:T(8,128)S(1)} %get-tuple-element.77.refs_2_.zl), channel_id=1, source_target_pairs={{1,0},{2,1},{3,2},{4,3},{5,4},{6,5},{7,6},{0,7},{9,8},{10,9},{11,1... | collective-permute-start | bytes 4718600 | tf_op jit(solution)/shard_map/ppermute | solution.py:32
  42.8 36.1 %collective-permute-start.8 = (f32[2,768,256]{2,1,0:T(8,128)S(1)}, f32[2,768,256]{2,1,0:T(8,128)S(1)}, u32[]{:S(2)}, u32[]{:S(2)}) collective-permute-start(f32[2,768,256]{2,1,0:T(8,128)S(1)} %get-tuple-element.79.refs_4_.zr), channel_id=1, source_target_pairs={{7,0},{0,1},{1,2},{2,3},{3,4},{4,5},{5,6},{6,7},{15,8},{8,9},{9,10... | collective-permute-start | bytes 4718600 | tf_op jit(solution)/shard_map/ppermute | solution.py:32
  42.8 36.1 %collective-permute-start.9 = (f32[3,256,256]{2,1,0:T(8,128)S(1)}, f32[3,256,256]{2,1,0:T(8,128)S(1)}, u32[]{:S(2)}, u32[]{:S(2)}) collective-permute-start(f32[3,256,256]{2,1,0:T(8,128)S(1)} %get-tuple-element.73.dn), channel_id=1, source_target_pairs={{120,0},{0,8},{8,16},{16,24},{24,32},{32,40},{40,48},{48,56},{56,6... | collective-permute-start | bytes 2359304 | tf_op jit(solution)/shard_map/ppermute | solution.py:32
  42.8 36.1 %collective-permute-start.11 = (f32[3,256,256]{2,1,0:T(8,128)S(1)}, f32[3,256,256]{2,1,0:T(8,128)S(1)}, u32[]{:S(2)}, u32[]{:S(2)}) collective-permute-start(f32[3,256,256]{2,1,0:T(8,128)S(1)} %get-tuple-element.74.up), channel_id=1, source_target_pairs={{8,0},{16,8},{24,16},{32,24},{40,32},{48,40},{56,48},{64,56},{72,6... | collective-permute-start | bytes 2359304 | tf_op jit(solution)/shard_map/ppermute | solution.py:32
  79.2 37.7 %collective-permute-start.12 = (f32[2,2,256,256]{3,2,1,0:T(8,128)S(1)}, f32[2,2,256,256]{3,2,1,0:T(8,128)S(1)}, u32[]{:S(2)}, u32[]{:S(2)}) collective-permute-start(f32[2,2,256,256]{3,2,1,0:T(8,128)S(1)} %get-tuple-element.81), channel_id=1, source_target_pairs={{8,0},{16,8},{24,16},{32,24},{40,32},{48,40},{56,48},{64,56},{72,6... | collective-permute-start | bytes 3145736 | tf_op jit(solution)/shard_map/ppermute | solution.py:32
  81.5 35.4 %collective-permute-start.13 = (f32[2,2,256,256]{3,2,1,0:T(8,128)S(1)}, f32[2,2,256,256]{3,2,1,0:T(8,128)S(1)}, u32[]{:S(2)}, u32[]{:S(2)}) collective-permute-start(f32[2,2,256,256]{3,2,1,0:T(8,128)S(1)} %get-tuple-element.82), channel_id=1, source_target_pairs={{120,0},{0,8},{8,16},{16,24},{24,32},{32,40},{40,48},{48,56},{56,6... | collective-permute-start | bytes 3145736 | tf_op jit(solution)/shard_map/ppermute | solution.py:32
  124.9 35.9 %collective-permute-start.16 = (f32[2,768,256]{2,1,0:T(8,128)S(1)}, f32[2,768,256]{2,1,0:T(8,128)S(1)}, u32[]{:S(2)}, u32[]{:S(2)}) collective-permute-start(f32[2,768,256]{2,1,0:T(8,128)S(1)} %get-tuple-element.98.refs_2_.zl), channel_id=1, source_target_pairs={{1,0},{2,1},{3,2},{4,3},{5,4},{6,5},{7,6},{0,7},{9,8},{10,9},{11,1... | collective-permute-start | bytes 4718600 | tf_op jit(solution)/shard_map/ppermute | solution.py:32
  125.8 35.0 %collective-permute-start.14 = (f32[2,768,256]{2,1,0:T(8,128)S(1)}, f32[2,768,256]{2,1,0:T(8,128)S(1)}, u32[]{:S(2)}, u32[]{:S(2)}) collective-permute-start(f32[2,768,256]{2,1,0:T(8,128)S(1)} %get-tuple-element.100.refs_4_.zr), channel_id=1, source_target_pairs={{7,0},{0,1},{1,2},{2,3},{3,4},{4,5},{5,6},{6,7},{15,8},{8,9},{9,10... | collective-permute-start | bytes 4718600 | tf_op jit(solution)/shard_map/ppermute | solution.py:32
  126.6 34.2 %collective-permute-start.15 = (f32[3,256,256]{2,1,0:T(8,128)S(1)}, f32[3,256,256]{2,1,0:T(8,128)S(1)}, u32[]{:S(2)}, u32[]{:S(2)}) collective-permute-start(f32[3,256,256]{2,1,0:T(8,128)S(1)} %get-tuple-element.94.dn), channel_id=1, source_target_pairs={{120,0},{0,8},{8,16},{16,24},{24,32},{32,40},{40,48},{48,56},{56,6... | collective-permute-start | bytes 2359304 | tf_op jit(solution)/shard_map/ppermute | solution.py:32
  126.6 34.2 %collective-permute-start.17 = (f32[3,256,256]{2,1,0:T(8,128)S(1)}, f32[3,256,256]{2,1,0:T(8,128)S(1)}, u32[]{:S(2)}, u32[]{:S(2)}) collective-permute-start(f32[3,256,256]{2,1,0:T(8,128)S(1)} %get-tuple-element.95.up), channel_id=1, source_target_pairs={{8,0},{16,8},{24,16},{32,24},{40,32},{48,40},{56,48},{64,56},{72,6... | collective-permute-start | bytes 2359304 | tf_op jit(solution)/shard_map/ppermute | solution.py:32
  161.2 39.5 %collective-permute-start.18 = (f32[2,2,256,256]{3,2,1,0:T(8,128)S(1)}, f32[2,2,256,256]{3,2,1,0:T(8,128)S(1)}, u32[]{:S(2)}, u32[]{:S(2)}) collective-permute-start(f32[2,2,256,256]{3,2,1,0:T(8,128)S(1)} %get-tuple-element.102), channel_id=1, source_target_pairs={{8,0},{16,8},{24,16},{32,24},{40,32},{48,40},{56,48},{64,56},{72,6... | collective-permute-start | bytes 3145736 | tf_op jit(solution)/shard_map/ppermute | solution.py:32
  165.6 35.1 %collective-permute-start.19 = (f32[2,2,256,256]{3,2,1,0:T(8,128)S(1)}, f32[2,2,256,256]{3,2,1,0:T(8,128)S(1)}, u32[]{:S(2)}, u32[]{:S(2)}) collective-permute-start(f32[2,2,256,256]{3,2,1,0:T(8,128)S(1)} %get-tuple-element.103), channel_id=1, source_target_pairs={{120,0},{0,8},{8,16},{16,24},{24,32},{32,40},{40,48},{48,56},{56,6... | collective-permute-start | bytes 3145736 | tf_op jit(solution)/shard_map/ppermute | solution.py:32
  208.9 34.4 %collective-permute-start.20 = (f32[2,768,256]{2,1,0:T(8,128)S(1)}, f32[2,768,256]{2,1,0:T(8,128)S(1)}, u32[]{:S(2)}, u32[]{:S(2)}) collective-permute-start(f32[2,768,256]{2,1,0:T(8,128)S(1)} %get-tuple-element.113), channel_id=1, source_target_pairs={{7,0},{0,1},{1,2},{2,3},{3,4},{4,5},{5,6},{6,7},{15,8},{8,9},{9,10... | collective-permute-start | bytes 4718600 | tf_op jit(solution)/shard_map/ppermute | solution.py:32
  209.7 33.6 %collective-permute-start.21 = (f32[3,256,256]{2,1,0:T(8,128)S(1)}, f32[3,256,256]{2,1,0:T(8,128)S(1)}, u32[]{:S(2)}, u32[]{:S(2)}) collective-permute-start(f32[3,256,256]{2,1,0:T(8,128)S(1)} %get-tuple-element.115), channel_id=1, source_target_pairs={{120,0},{0,8},{8,16},{16,24},{24,32},{32,40},{40,48},{48,56},{56,6... | collective-permute-start | bytes 2359304 | tf_op jit(solution)/shard_map/ppermute | solution.py:32
  244.0 26.0 %collective-permute-start.22 = (f32[1,2,256,256]{3,2,1,0:T(8,128)S(1)}, f32[1,2,256,256]{3,2,1,0:T(8,128)S(1)}, u32[]{:S(2)}, u32[]{:S(2)}) collective-permute-start(f32[1,2,256,256]{3,2,1,0:T(8,128)S(1)} %get-tuple-element.120), channel_id=1, source_target_pairs={{120,0},{0,8},{8,16},{16,24},{24,32},{32,40},{40,48},{48,56},{56,6... | collective-permute-start | bytes 1572872 | tf_op jit(solution)/shard_map/ppermute | solution.py:32
where the time goes:
time: 276 us; the launch traced here: 272 us
  blocking collectives  190 us (69%)
  starting transfers between devices  36.8 us (13%)
  Pallas kernels  26.6 us (10%)
  waiting for transfers between devices  15.4 us (6%)
    all_to_all x6, blocking collectives, everyone(): return lax.all_to_all(x, ('row', 'col'), 0, 0)  190 us
    ppermute x23, starting transfers between devices, passed_along(): return lax.ppermute(block, axis, route)  36.8 us
    pallas_call x8, Pallas kernels, call(): pl.pallas_call(kernel, out_shape=tuple(outs), in_specs=[SMEM if i in smem...  26.6 us
    ppermute x23, waiting for transfers between devices, passed_along(): return lax.ppermute(block, axis, route)  15.4 us
  transfers between devices with their start and end apart: 23, of which 3 were waited for; matrix products, arithmetic and copies ran while one was open for 0% of the time, Pallas kernels for 0%

commit v1 on v0

--- a/solution.py
+++ b/solution.py
@@ -169,12 +169,18 @@
     lax.fori_loop(pairs * BESIDE, n, more, 0)
 
 
+def on_left_core():
+    return lax.rem(lax.axis_index("col"), 2) == 0
+
+
 def hand_out(canvas, grads, zl_out, zr_out, up_out, mid_out, dn_out, g_out):
     zl_out[...] = canvas[:, :, :F]
     zr_out[...] = canvas[:, :, TILE:]
     up_out[:2] = canvas[:, :F, F:TILE]
+    up_out[2] = jnp.where(on_left_core(), canvas[0, :F, TILE:], canvas[0, :F, :F])
     mid_out[...] = canvas[:, F:TILE, F:TILE]
     dn_out[:2] = canvas[:, TILE:, F:TILE]
+    dn_out[2] = jnp.where(on_left_core(), canvas[0, TILE:, TILE:], canvas[0, TILE:, :F])
     for p in range(3):
         for h in range(2):
             for t in range(2):
@@ -212,7 +218,7 @@
                 pr[p, h * HALF : (h + 1) * HALF, t * LANES : (t + 1) * LANES] = pg[pl.ds(4 * p + 2 * t + h, HALF, stride=8), :]
 
 
-def refreshed(put, size, o, l, zl, zr, up, mid, dn, left_in, right_in, cup, cdn, sup, sdn):
+def refreshed(put, size, o, l, zl, zr, up, mid, dn, left_in, right_in, across):
     for i in range(size // F):
         for j in range(size // F):
             for at in range(0, F, STRIP):
@@ -226,20 +232,28 @@
                         s = (up, mid, dn)[i][p, here, :]
                     else:
                         s = zr[p, rows, :] + right_in[p, rows, :]
-                    if i == 0:
-                        s = s + (cdn[p, here, :] if j == 1 else sdn[j // 2, p, here, :])
-                    if i == 2:
-                        s = s + (cup[p, here, :] if j == 1 else sup[j // 2, p, here, :])
+                    if i != 1:
+                        s = s + across(i, j, p, here)
                     put(p, rows, cols, o[p, rows, cols] + s * scale)
 
 
-def next_kernel(mine, ia, ib, ic, amp, left, right, pg, o, l, zl, zr, up, mid, dn, left_in, right_in, cup, cdn, sup, sdn, *rest):
+def next_kernel(mine, ia, ib, ic, amp, left, right, pg, o, l, zl, zr, up, mid, dn, left_in, right_in, cup, cdn, sup, sdn, swap, *rest):
     ob, light, outs, (pr, canvas, grads, listed, glow) = rest[0], rest[1], rest[2:8], rest[8:]
 
     def put(p, rows, cols, value):
         ob[p, rows, cols] = value
 
-    refreshed(put, WIDE, o, l, zl, zr, up, mid, dn, left_in, right_in, cup, cdn, sup, sdn)
+    left_core = on_left_core()
+
+    def across(i, j, p, here):
+        centre, side = (cdn, sdn) if i == 0 else (cup, sup)
+        if j == 1:
+            return centre[p, here, :]
+        outer = side[p, here, :]
+        inner = centre[2, here, :] + swap[i // 2, here, :] if p == 0 else side[2, here, :]
+        return jnp.where(left_core == (j == 2), inner, outer)
+
+    refreshed(put, WIDE, o, l, zl, zr, up, mid, dn, left_in, right_in, across)
     gathered_probe(pg, pr)
     visit_frames(mine, (ia, ib, ic), amp, left, right, ob, pr, canvas, glow, grads, listed)
     light[...] = glow[F : F + WIDE, F : F + WIDE]
@@ -250,7 +264,10 @@
     def put(p, rows, cols, value):
         o_out[p, rows, cols] = value
 
-    refreshed(put, TILE, o, l, zl, None, up, mid, None, left_in, None, None, cdn, None, sdn)
+    def across(i, j, p, here):
+        return cdn[p, here, :] if j == 1 else sdn[0, p, here, :]
+
+    refreshed(put, TILE, o, l, zl, None, up, mid, None, left_in, None, across)
     gathered_probe(pg, p_out)
 
 
@@ -259,11 +276,17 @@
         sdn, new, spread = rest
         sdn[0] = zl[:, TILE:] + left_in[:, TILE:]
     else:
-        zr, right_in, sup, sdn, new, spread = rest
-        sup[0] = zl[:, :F] + left_in[:, :F]
-        sup[1] = zr[:, :F] + right_in[:, :F]
-        sdn[0] = zl[:, TILE:] + left_in[:, TILE:]
-        sdn[1] = zr[:, TILE:] + right_in[:, TILE:]
+        zr, right_in, cup, cdn, sup, sdn, swap, new, spread = rest
+        left_core = on_left_core()
+        for out, rows in ((sup, slice(0, F)), (sdn, slice(TILE, WIDE))):
+            for p in range(2):
+                a = zl[p, rows] + left_in[p, rows]
+                b = zr[p, rows] + right_in[p, rows]
+                out[p] = jnp.where(left_core, a, b)
+                if p == 1:
+                    out[2] = jnp.where(left_core, b, a)
+        swap[0] = cdn[2]
+        swap[1] = cup[2]
     s = jnp.sum(g[...].reshape(HALF // 2, 24, LANES), axis=0)
     s = s[:12] + s[12:]
     value = old[...] + s[:8] / (jnp.concatenate([s[8:], s[8:]], 0) + probe_damping)
@@ -347,12 +370,14 @@
             moved = (passed_along(side_down, "row", 1),)
         else:
             from_left, centre_down, from_right, centre_up = moved
-            side_up, side_down, own, spread = call(
-                lambda *refs: middle_kernel(False, *refs), (grad, own, to_left, from_left, to_right, from_right),
-                (f32(2, 2, F, F), f32(2, 2, F, F)) + tail,
+            side_up, side_down, swap, own, spread = call(
+                lambda *refs: middle_kernel(False, *refs),
+                (grad, own, to_left, from_left, to_right, from_right, centre_up, centre_down),
+                (f32(3, F, F), f32(3, F, F), f32(2, F, F)) + tail,
             )
-            sides = (side_up, side_down)
-            moved = (passed_along(side_up, "row", -1), passed_along(side_down, "row", 1))
+            sides = (side_up, side_down, swap)
+            swapped = lax.ppermute(swap, "col", [(i, i ^ 1) for i in range(lax.axis_size("col"))])
+            moved = (passed_along(side_up, "row", -1), passed_along(side_down, "row", 1), swapped)
         sides, spread = lax.optimization_barrier((sides, spread))
         pg = everyone(spread.reshape(HALF, 2, 4, LANES)).reshape(HALF * 8, LANES)
         if last:
@@ -362,7 +387,7 @@
             )
         state = call_frames(
             next_kernel, mine, *infos, amp, left, right, pg, ob, light, to_left, to_right, up, mid, down,
-            from_left, from_right, centre_up, centre_down, moved[0], moved[1], alias={8: 0},
+            from_left, from_right, centre_up, centre_down, *moved, alias={8: 0},
         )
 
 

time: 276 us -> 268 us (0.971); the launches traced: 272 us -> 267 us
  blocking collectives: 190 us -> 179 us
  starting transfers between devices: 36.8 us -> 42.6 us
    all_to_all x6, blocking collectives: 190 us -> 179 us  [everyone(): return lax.all_to_all(x, ('row', 'col'), 0, 0)]
    ppermute x23, starting transfers between devices: 36.8 us -> 41.2 us  [passed_along(): return lax.ppermute(block, axis, route)]
  transfers between devices with their start and end apart: 23 -> 25, of which waited for: 3 -> 3; matrix products, arithmetic and copies ran while one was open for 0% -> 0% of each run, Pallas kernels for 0% -> 0%
where the time goes in v1:
time: 268 us; the launch traced here: 267 us
  blocking collectives  179 us (67%)
  starting transfers between devices  42.6 us (16%)
  Pallas kernels  26.9 us (10%)
  waiting for transfers between devices  15.4 us (6%)
    all_to_all x6, blocking collectives, everyone(): return lax.all_to_all(x, ('row', 'col'), 0, 0)  179 us
    ppermute x23, starting transfers between devices, passed_along(): return lax.ppermute(block, axis, route)  41.2 us
    pallas_call x8, Pallas kernels, call(): pl.pallas_call(kernel, out_shape=tuple(outs), in_specs=[SMEM if i in smem...  26.9 us
    ppermute x23, waiting for transfers between devices, passed_along(): return lax.ppermute(block, axis, route)  15.4 us
  transfers between devices with their start and end apart: 25, of which 3 were waited for; matrix products, arithmetic and copies ran while one was open for 0% of the time, Pallas kernels for 0%

profile of v1, /device:TPU:1, one launch (start us, length us, event | category | flops | bytes accessed | tf_op | source)
XLA Modules:
  0.0 267.3 jit_solution(8658156705105382731)
XLA Ops:
  0.6 1.5 fusion
  2.1 0.0 copy-start.5
  2.1 0.0 copy-start.4
  2.1 5.8 %collective-permute-start = (f32[2,256,256]{2,1,0:T(8,128)S(1)}, f32[2,256,256]{2,1,0:T(8,128)S(1)}, u32[]{:S(2)}, u32[]{:S(2)}) collective-permute-start(f32[2,256,256]{2,1,0:T(8,128)S(1)} %get-tuple-element.133), channel_id=1, source_target_pairs={{8,0},{16,8},{24,16},{32,24},{40,32},{48,40},{56,48},{64,56},{72,6... | collective-permute-start | bytes 1572872 | tf_op jit(solution)/shard_map/ppermute | solution.py:32
  8.0 0.1 slice.19
  8.1 0.0 copy-start
  8.1 0.0 copy-start.2
  8.1 1.0 collective-permute-start.6
  9.9 0.1 add_bitcast_fusion.mine
  10.0 3.0 %collective-permute-start.2 = (s32[1,16]{1,0:T(1,128)S(1)}, s32[1,16]{1,0:T(1,128)S(1)}, u32[]{:S(2)}, u32[]{:S(2)}) collective-permute-start(s32[1,16]{1,0:T(1,128)S(1)} %add_bitcast_fusion.mine), channel_id=1, source_target_pairs={{1,0},{2,1},{3,2},{4,3},{5,4},{6,5},{7,6},{0,7},{9,8},{10,9},{11,1... | collective-permute-start | bytes 200 | tf_op jit(solution)/shard_map/ppermute | solution.py:32
  13.0 0.0 collective-permute-start.1
  13.0 0.5 collective-permute-start.5
  13.6 9.8 %collective-permute-done.2 = s32[1,16]{1,0:T(1,128)S(1)} collective-permute-done((s32[1,16]{1,0:T(1,128)S(1)}, s32[1,16]{1,0:T(1,128)S(1)}, u32[]{:S(2)}, u32[]{:S(2)}) %collective-permute-start.2) | collective-permute-done | bytes 96 | tf_op jit(solution)/shard_map/ppermute | solution.py:32
  23.4 0.0 collective-permute-done.1
  23.4 0.0 collective-permute-done.below
  23.4 1.3 collective-permute-start.7
  24.6 2.1 collective-permute-start.4
  26.8 0.0 collective-permute-start.3
  26.8 0.2 shard_map.86
  27.0 2.8 %collective-permute-done.5.below_right = f32[2,256,256]{2,1,0:T(8,128)S(1)} collective-permute-done((f32[2,256,256]{2,1,0:T(8,128)S(1)}, f32[2,256,256]{2,1,0:T(8,128)S(1)}, u32[]{:S(2)}, u32[]{:S(2)}) %collective-permute-start.5) | collective-permute-done | bytes 524320 | tf_op jit(solution)/shard_map/ppermute | solution.py:32
  29.8 0.0 collective-permute-done.4.ic
  29.8 2.7 %collective-permute-done.3.ia = s32[3,16]{1,0:T(4,128)S(1)} collective-permute-done((s32[3,16]{1,0:T(4,128)S(1)}, s32[3,16]{1,0:T(4,128)S(1)}, u32[]{:S(2)}, u32[]{:S(2)}) %collective-permute-start.3) | collective-permute-done | bytes 224 | tf_op jit(solution)/shard_map/ppermute | solution.py:32
  32.5 7.0 %shard_map.87 = (f32[2,768,768]{2,1,0:T(8,128)S(1)}, f32[768,768]{1,0:T(8,128)S(1)}, f32[2,768,256]{2,1,0:T(8,128)S(1)}, f32[2,768,256]{2,1,0:T(8,128)S(1)}, f32...) custom-call(s32[1,16]{1,0:T(1,128)S(1)} %add_bitcast_fusion.mine, ...), custom_call_target="tpu_custom_call", output_to_operand_aliasing={{0}: (8, {})} | custom-call | tf_op jit(solution)/shard_map/pallas_call | solution.py:302
  39.5 3.2 %collective-permute-start.10 = (f32[2,768,256]{2,1,0:T(8,128)S(1)}, f32[2,768,256]{2,1,0:T(8,128)S(1)}, u32[]{:S(2)}, u32[]{:S(2)}) collective-permute-start(f32[2,768,256]{2,1,0:T(8,128)S(1)} %get-tuple-element.79.refs_2_.zl), channel_id=1, source_target_pairs={{1,0},{2,1},{3,2},{4,3},{5,4},{6,5},{7,6},{0,7},{9,8},{10,9},{11,1... | collective-permute-start | bytes 4718600 | tf_op jit(solution)/shard_map/ppermute | solution.py:32
  42.8 4.8 %collective-permute-start.11 = (f32[3,256,256]{2,1,0:T(8,128)S(1)}, f32[3,256,256]{2,1,0:T(8,128)S(1)}, u32[]{:S(2)}, u32[]{:S(2)}) collective-permute-start(f32[3,256,256]{2,1,0:T(8,128)S(1)} %get-tuple-element.76.up), channel_id=1, source_target_pairs={{8,0},{16,8},{24,16},{32,24},{40,32},{48,40},{56,48},{64,56},{72,6... | collective-permute-start | bytes 2359304 | tf_op jit(solution)/shard_map/ppermute | solution.py:32
  47.6 31.6 %all_to_all.30 = f32[128,3,4,128]{3,2,1,0:T(4,128)S(1)} all-to-all(f32[128,3,4,128]{3,2,1,0:T(4,128)S(1)} %bitcast.32), channel_id=1, replica_groups=mesh['row'=16,'col'=8] {'row','col'}, dimensions={0} | all-to-all | bytes 1572864 | tf_op jit(solution)/shard_map/all_to_all | solution.py:330
  79.2 0.0 collective-permute-done.9.refs_7_.cdn
  79.2 0.0 collective-permute-done.11.refs_6_.cup
  79.2 0.0 collective-permute-done.10.refs_5_.right_in
  79.2 0.3 shard_map.88
  79.5 5.6 %collective-permute-start.12 = (f32[3,256,256]{2,1,0:T(8,128)S(1)}, f32[3,256,256]{2,1,0:T(8,128)S(1)}, u32[]{:S(2)}, u32[]{:S(2)}) collective-permute-start(f32[3,256,256]{2,1,0:T(8,128)S(1)} %get-tuple-element.85), channel_id=1, source_target_pairs={{8,0},{16,8},{24,16},{32,24},{40,32},{48,40},{56,48},{64,56},{72,6... | collective-permute-start | bytes 2359304 | tf_op jit(solution)/shard_map/ppermute | solution.py:32
  85.1 0.7 collective-permute-start.14
  85.8 27.7 %all_to_all.31 = f32[128,2,4,128]{3,2,1,0:T(4,128)S(1)} all-to-all(f32[128,2,4,128]{3,2,1,0:T(4,128)S(1)} %bitcast.33), channel_id=1, replica_groups=mesh['row'=16,'col'=8] {'row','col'}, dimensions={0} | all-to-all | bytes 1048576 | tf_op jit(solution)/shard_map/all_to_all | solution.py:330
  113.4 8.0 %shard_map.89 = (f32[2,768,768]{2,1,0:T(8,128)S(1)}, f32[768,768]{1,0:T(8,128)S(1)}, f32[2,768,256]{2,1,0:T(8,128)S(1)}, f32[2,768,256]{2,1,0:T(8,128)S(1)}, f32...) custom-call(s32[1,16]{1,0:T(1,128)S(1)} %add_bitcast_fusion.mine, ...), custom_call_target="tpu_custom_call", output_to_operand_aliasing={{0}: (8, {})} | custom-call | tf_op jit(solution)/shard_map/pallas_call | solution.py:302
  121.5 0.4 collective-permute-start.17
  121.9 1.4 collective-permute-start.15
  123.2 4.8 %collective-permute-start.18 = (f32[3,256,256]{2,1,0:T(8,128)S(1)}, f32[3,256,256]{2,1,0:T(8,128)S(1)}, u32[]{:S(2)}, u32[]{:S(2)}) collective-permute-start(f32[3,256,256]{2,1,0:T(8,128)S(1)} %get-tuple-element.98.up), channel_id=1, source_target_pairs={{8,0},{16,8},{24,16},{32,24},{40,32},{48,40},{56,48},{64,56},{72,6... | collective-permute-start | bytes 2359304 | tf_op jit(solution)/shard_map/ppermute | solution.py:32
  128.0 32.7 %all_to_all.32 = f32[128,3,4,128]{3,2,1,0:T(4,128)S(1)} all-to-all(f32[128,3,4,128]{3,2,1,0:T(4,128)S(1)} %bitcast.30), channel_id=1, replica_groups=mesh['row'=16,'col'=8] {'row','col'}, dimensions={0} | all-to-all | bytes 1572864 | tf_op jit(solution)/shard_map/all_to_all | solution.py:330
  160.7 0.3 shard_map.90
  161.1 6.0 %collective-permute-start.19 = (f32[3,256,256]{2,1,0:T(8,128)S(1)}, f32[3,256,256]{2,1,0:T(8,128)S(1)}, u32[]{:S(2)}, u32[]{:S(2)}) collective-permute-start(f32[3,256,256]{2,1,0:T(8,128)S(1)} %get-tuple-element.107), channel_id=1, source_target_pairs={{8,0},{16,8},{24,16},{32,24},{40,32},{48,40},{56,48},{64,56},{72,6... | collective-permute-start | bytes 2359304 | tf_op jit(solution)/shard_map/ppermute | solution.py:32
  167.0 0.7 collective-permute-start.21
  167.7 28.0 %all_to_all.33 = f32[128,2,4,128]{3,2,1,0:T(4,128)S(1)} all-to-all(f32[128,2,4,128]{3,2,1,0:T(4,128)S(1)} %bitcast.34), channel_id=1, replica_groups=mesh['row'=16,'col'=8] {'row','col'}, dimensions={0} | all-to-all | bytes 1048576 | tf_op jit(solution)/shard_map/all_to_all | solution.py:330
  195.7 8.2 %shard_map.91 = (f32[2,768,768]{2,1,0:T(8,128)S(1)}, f32[768,768]{1,0:T(8,128)S(1)}, f32[2,768,256]{2,1,0:T(8,128)S(1)}, f32[2,768,256]{2,1,0:T(8,128)S(1)}, f32...) custom-call(s32[1,16]{1,0:T(1,128)S(1)} %add_bitcast_fusion.mine, ...), custom_call_target="tpu_custom_call", output_to_operand_aliasing={{0}: (8, {})} | custom-call | tf_op jit(solution)/shard_map/pallas_call | solution.py:302
  203.9 1.3 collective-permute-start.22
  205.3 37.1 %all_to_all.34 = f32[128,3,4,128]{3,2,1,0:T(4,128)S(1)} all-to-all(f32[128,3,4,128]{3,2,1,0:T(4,128)S(1)} %bitcast.31), channel_id=1, replica_groups=mesh['row'=16,'col'=8] {'row','col'}, dimensions={0} | all-to-all | bytes 1572864 | tf_op jit(solution)/shard_map/all_to_all | solution.py:330
  242.3 0.7 shard_map.92
  243.0 22.2 %all_to_all.35 = f32[128,2,4,128]{3,2,1,0:T(4,128)S(1)} all-to-all(f32[128,2,4,128]{3,2,1,0:T(4,128)S(1)} %bitcast.35), channel_id=1, replica_groups=mesh['row'=16,'col'=8] {'row','col'}, dimensions={0} | all-to-all | bytes 1048576 | tf_op jit(solution)/shard_map/all_to_all | solution.py:330
  265.3 2.0 shard_map.93
  (34 shorter events, 0.1 us)
Async XLA Ops:
  0.6 7.3 %copy-start.3 = (f32[2,512,512]{2,1,0:T(8,128)S(1)}, f32[2,512,512]{2,1,0:T(8,128)}, u32[]{:S(2)}) copy-start(f32[2,512,512]{2,1,0:T(8,128)} %tile.1) | copy-start | bytes 6291460
  2.1 7.8 %copy-start.5 = (s32[1,1,4,2]{2,3,1,0:T(2,128)S(1)}, s32[1,1,4,2]{2,3,1,0:T(2,128)}, u32[]{:S(2)}) copy-start(s32[1,1,4,2]{2,3,1,0:T(2,128)} %param.10) | copy-start | bytes 100
  2.1 24.7 %copy-start.4 = (f32[2,256,256]{2,1,0:T(8,128)S(1)}, f32[2,256,256]{2,1,0:T(8,128)}, u32[]{:S(2)}) copy-start(f32[2,256,256]{2,1,0:T(8,128)} %probe.1) | copy-start | bytes 1572868
  2.1 21.3 %collective-permute-start = (f32[2,256,256]{2,1,0:T(8,128)S(1)}, f32[2,256,256]{2,1,0:T(8,128)S(1)}, u32[]{:S(2)}, u32[]{:S(2)}) collective-permute-start(f32[2,256,256]{2,1,0:T(8,128)S(1)} %get-tuple-element.133), channel_id=1, source_target_pairs={{8,0},{16,8},{24,16},{32,24},{40,32},{48,40},{56,48},{64,56},{72,6... | collective-permute-start | bytes 1572872 | tf_op jit(solution)/shard_map/ppermute | solution.py:32
  8.0 24.6 %copy-start.1 = (bf16[512,1536]{1,0:T(8,128)(2,1)S(1)}, bf16[512,1536]{1,0:T(8,128)(2,1)}, u32[]{:S(2)}) copy-start(bf16[512,1536]{1,0:T(8,128)(2,1)} %constant.6.clone.left) | copy-start | bytes 4718596
  8.1 24.5 %copy-start = (bf16[1536,512]{1,0:T(8,128)(2,1)S(1)}, bf16[1536,512]{1,0:T(8,128)(2,1)}, u32[]{:S(2)}) copy-start(bf16[1536,512]{1,0:T(8,128)(2,1)} %constant.7.clone.right) | copy-start | bytes 4718596
  8.1 24.5 %copy-start.2 = (f32[1,1,4,256,256]{4,3,2,1,0:T(8,128)S(1)}, f32[1,1,4,256,256]{4,3,2,1,0:T(8,128)}, u32[]{:S(2)}) copy-start(f32[1,1,4,256,256]{4,3,2,1,0:T(8,128)} %param.9) | copy-start | bytes 3145732
  8.1 24.4 %collective-permute-start.6 = (f32[2,512,256]{2,1,0:T(8,128)S(1)}, f32[2,512,256]{2,1,0:T(8,128)S(1)}, u32[]{:S(2)}, u32[]{:S(2)}) collective-permute-start(f32[2,512,256]{2,1,0:T(8,128)S(1)} %slice.19), channel_id=1, source_target_pairs={{1,0},{2,1},{3,2},{4,3},{5,4},{6,5},{7,6},{0,7},{9,8},{10,9},{11,1... | collective-permute-start | bytes 3145736 | tf_op jit(solution)/shard_map/ppermute | solution.py:32
  10.0 13.4 %collective-permute-start.2 = (s32[1,16]{1,0:T(1,128)S(1)}, s32[1,16]{1,0:T(1,128)S(1)}, u32[]{:S(2)}, u32[]{:S(2)}) collective-permute-start(s32[1,16]{1,0:T(1,128)S(1)} %add_bitcast_fusion.mine), channel_id=1, source_target_pairs={{1,0},{2,1},{3,2},{4,3},{5,4},{6,5},{7,6},{0,7},{9,8},{10,9},{11,1... | collective-permute-start | bytes 200 | tf_op jit(solution)/shard_map/ppermute | solution.py:32
  13.0 10.3 %collective-permute-start.1 = (s32[1,16]{1,0:T(1,128)S(1)}, s32[1,16]{1,0:T(1,128)S(1)}, u32[]{:S(2)}, u32[]{:S(2)}) collective-permute-start(s32[1,16]{1,0:T(1,128)S(1)} %add_bitcast_fusion.mine), channel_id=1, source_target_pairs={{7,0},{0,1},{1,2},{2,3},{3,4},{4,5},{5,6},{6,7},{15,8},{8,9},{9,10... | collective-permute-start | bytes 200 | tf_op jit(solution)/shard_map/ppermute | solution.py:32
  13.0 16.8 %collective-permute-start.5 = (f32[2,256,256]{2,1,0:T(8,128)S(1)}, f32[2,256,256]{2,1,0:T(8,128)S(1)}, u32[]{:S(2)}, u32[]{:S(2)}) collective-permute-start(f32[2,256,256]{2,1,0:T(8,128)S(1)} %get-tuple-element.132), channel_id=1, source_target_pairs={{8,0},{16,8},{24,16},{32,24},{40,32},{48,40},{56,48},{64,56},{72,6... | collective-permute-start | bytes 1572872 | tf_op jit(solution)/shard_map/ppermute | solution.py:32
  23.4 9.1 %collective-permute-start.7 = (f32[2,256,256]{2,1,0:T(8,128)S(1)}, f32[2,256,256]{2,1,0:T(8,128)S(1)}, u32[]{:S(2)}, u32[]{:S(2)}) collective-permute-start(f32[2,256,256]{2,1,0:T(8,128)S(1)} %collective-permute-done.below), channel_id=1, source_target_pairs={{1,0},{2,1},{3,2},{4,3},{5,4},{6,5},{7,6},{0,7},{9,8},{10,9},{11,1... | collective-permute-start | bytes 1572872 | tf_op jit(solution)/shard_map/ppermute | solution.py:32
  24.6 5.2 %collective-permute-start.4 = (s32[3,16]{1,0:T(4,128)S(1)}, s32[3,16]{1,0:T(4,128)S(1)}, u32[]{:S(2)}, u32[]{:S(2)}) collective-permute-start(s32[3,16]{1,0:T(4,128)S(1)} %pad_add_fusion.ib), channel_id=1, source_target_pairs={{8,0},{16,8},{24,16},{32,24},{40,32},{48,40},{56,48},{64,56},{72,6... | collective-permute-start | bytes 584 | tf_op jit(solution)/shard_map/ppermute | solution.py:32
  26.8 5.8 %collective-permute-start.3 = (s32[3,16]{1,0:T(4,128)S(1)}, s32[3,16]{1,0:T(4,128)S(1)}, u32[]{:S(2)}, u32[]{:S(2)}) collective-permute-start(s32[3,16]{1,0:T(4,128)S(1)} %pad_add_fusion.ib), channel_id=1, source_target_pairs={{120,0},{0,8},{8,16},{16,24},{24,32},{32,40},{40,48},{48,56},{56,6... | collective-permute-start | bytes 584 | tf_op jit(solution)/shard_map/ppermute | solution.py:32
  39.5 39.6 %collective-permute-start.10 = (f32[2,768,256]{2,1,0:T(8,128)S(1)}, f32[2,768,256]{2,1,0:T(8,128)S(1)}, u32[]{:S(2)}, u32[]{:S(2)}) collective-permute-start(f32[2,768,256]{2,1,0:T(8,128)S(1)} %get-tuple-element.79.refs_2_.zl), channel_id=1, source_target_pairs={{1,0},{2,1},{3,2},{4,3},{5,4},{6,5},{7,6},{0,7},{9,8},{10,9},{11,1... | collective-permute-start | bytes 4718600 | tf_op jit(solution)/shard_map/ppermute | solution.py:32
  42.8 36.4 %collective-permute-start.8 = (f32[2,768,256]{2,1,0:T(8,128)S(1)}, f32[2,768,256]{2,1,0:T(8,128)S(1)}, u32[]{:S(2)}, u32[]{:S(2)}) collective-permute-start(f32[2,768,256]{2,1,0:T(8,128)S(1)} %get-tuple-element.81.refs_4_.zr), channel_id=1, source_target_pairs={{7,0},{0,1},{1,2},{2,3},{3,4},{4,5},{5,6},{6,7},{15,8},{8,9},{9,10... | collective-permute-start | bytes 4718600 | tf_op jit(solution)/shard_map/ppermute | solution.py:32
  42.8 36.4 %collective-permute-start.9 = (f32[3,256,256]{2,1,0:T(8,128)S(1)}, f32[3,256,256]{2,1,0:T(8,128)S(1)}, u32[]{:S(2)}, u32[]{:S(2)}) collective-permute-start(f32[3,256,256]{2,1,0:T(8,128)S(1)} %get-tuple-element.75.dn), channel_id=1, source_target_pairs={{120,0},{0,8},{8,16},{16,24},{24,32},{32,40},{40,48},{48,56},{56,6... | collective-permute-start | bytes 2359304 | tf_op jit(solution)/shard_map/ppermute | solution.py:32
  42.8 36.4 %collective-permute-start.11 = (f32[3,256,256]{2,1,0:T(8,128)S(1)}, f32[3,256,256]{2,1,0:T(8,128)S(1)}, u32[]{:S(2)}, u32[]{:S(2)}) collective-permute-start(f32[3,256,256]{2,1,0:T(8,128)S(1)} %get-tuple-element.76.up), channel_id=1, source_target_pairs={{8,0},{16,8},{24,16},{32,24},{40,32},{48,40},{56,48},{64,56},{72,6... | collective-permute-start | bytes 2359304 | tf_op jit(solution)/shard_map/ppermute | solution.py:32
  79.5 33.9 %collective-permute-start.12 = (f32[3,256,256]{2,1,0:T(8,128)S(1)}, f32[3,256,256]{2,1,0:T(8,128)S(1)}, u32[]{:S(2)}, u32[]{:S(2)}) collective-permute-start(f32[3,256,256]{2,1,0:T(8,128)S(1)} %get-tuple-element.85), channel_id=1, source_target_pairs={{8,0},{16,8},{24,16},{32,24},{40,32},{48,40},{56,48},{64,56},{72,6... | collective-permute-start | bytes 2359304 | tf_op jit(solution)/shard_map/ppermute | solution.py:32
  85.1 28.3 %collective-permute-start.13 = (f32[3,256,256]{2,1,0:T(8,128)S(1)}, f32[3,256,256]{2,1,0:T(8,128)S(1)}, u32[]{:S(2)}, u32[]{:S(2)}) collective-permute-start(f32[3,256,256]{2,1,0:T(8,128)S(1)} %get-tuple-element.86), channel_id=1, source_target_pairs={{120,0},{0,8},{8,16},{16,24},{24,32},{32,40},{40,48},{48,56},{56,6... | collective-permute-start | bytes 2359304 | tf_op jit(solution)/shard_map/ppermute | solution.py:32
  85.1 28.3 %collective-permute-start.14 = (f32[2,256,256]{2,1,0:T(8,128)S(1)}, f32[2,256,256]{2,1,0:T(8,128)S(1)}, u32[]{:S(2)}, u32[]{:S(2)}) collective-permute-start(f32[2,256,256]{2,1,0:T(8,128)S(1)} %get-tuple-element.87), channel_id=1, source_target_pairs={{0,1},{1,0},{2,3},{3,2},{4,5},{5,4},{6,7},{7,6},{8,9},{9,8},{10,11... | collective-permute-start | bytes 1572872 | tf_op jit(solution)/shard_map/ppermute | solution.py:379
  121.5 39.2 %collective-permute-start.17 = (f32[2,768,256]{2,1,0:T(8,128)S(1)}, f32[2,768,256]{2,1,0:T(8,128)S(1)}, u32[]{:S(2)}, u32[]{:S(2)}) collective-permute-start(f32[2,768,256]{2,1,0:T(8,128)S(1)} %get-tuple-element.101.refs_2_.zl), channel_id=1, source_target_pairs={{1,0},{2,1},{3,2},{4,3},{5,4},{6,5},{7,6},{0,7},{9,8},{10,9},{11,1... | collective-permute-start | bytes 4718600 | tf_op jit(solution)/shard_map/ppermute | solution.py:32
  121.9 38.8 %collective-permute-start.15 = (f32[2,768,256]{2,1,0:T(8,128)S(1)}, f32[2,768,256]{2,1,0:T(8,128)S(1)}, u32[]{:S(2)}, u32[]{:S(2)}) collective-permute-start(f32[2,768,256]{2,1,0:T(8,128)S(1)} %get-tuple-element.103.refs_4_.zr), channel_id=1, source_target_pairs={{7,0},{0,1},{1,2},{2,3},{3,4},{4,5},{5,6},{6,7},{15,8},{8,9},{9,10... | collective-permute-start | bytes 4718600 | tf_op jit(solution)/shard_map/ppermute | solution.py:32
  123.2 37.4 %collective-permute-start.16 = (f32[3,256,256]{2,1,0:T(8,128)S(1)}, f32[3,256,256]{2,1,0:T(8,128)S(1)}, u32[]{:S(2)}, u32[]{:S(2)}) collective-permute-start(f32[3,256,256]{2,1,0:T(8,128)S(1)} %get-tuple-element.97.dn), channel_id=1, source_target_pairs={{120,0},{0,8},{8,16},{16,24},{24,32},{32,40},{40,48},{48,56},{56,6... | collective-permute-start | bytes 2359304 | tf_op jit(solution)/shard_map/ppermute | solution.py:32
  123.2 37.4 %collective-permute-start.18 = (f32[3,256,256]{2,1,0:T(8,128)S(1)}, f32[3,256,256]{2,1,0:T(8,128)S(1)}, u32[]{:S(2)}, u32[]{:S(2)}) collective-permute-start(f32[3,256,256]{2,1,0:T(8,128)S(1)} %get-tuple-element.98.up), channel_id=1, source_target_pairs={{8,0},{16,8},{24,16},{32,24},{40,32},{48,40},{56,48},{64,56},{72,6... | collective-permute-start | bytes 2359304 | tf_op jit(solution)/shard_map/ppermute | solution.py:32
  161.1 34.6 %collective-permute-start.19 = (f32[3,256,256]{2,1,0:T(8,128)S(1)}, f32[3,256,256]{2,1,0:T(8,128)S(1)}, u32[]{:S(2)}, u32[]{:S(2)}) collective-permute-start(f32[3,256,256]{2,1,0:T(8,128)S(1)} %get-tuple-element.107), channel_id=1, source_target_pairs={{8,0},{16,8},{24,16},{32,24},{40,32},{48,40},{56,48},{64,56},{72,6... | collective-permute-start | bytes 2359304 | tf_op jit(solution)/shard_map/ppermute | solution.py:32
  167.0 28.7 %collective-permute-start.20 = (f32[3,256,256]{2,1,0:T(8,128)S(1)}, f32[3,256,256]{2,1,0:T(8,128)S(1)}, u32[]{:S(2)}, u32[]{:S(2)}) collective-permute-start(f32[3,256,256]{2,1,0:T(8,128)S(1)} %get-tuple-element.108), channel_id=1, source_target_pairs={{120,0},{0,8},{8,16},{16,24},{24,32},{32,40},{40,48},{48,56},{56,6... | collective-permute-start | bytes 2359304 | tf_op jit(solution)/shard_map/ppermute | solution.py:32
  167.0 28.6 %collective-permute-start.21 = (f32[2,256,256]{2,1,0:T(8,128)S(1)}, f32[2,256,256]{2,1,0:T(8,128)S(1)}, u32[]{:S(2)}, u32[]{:S(2)}) collective-permute-start(f32[2,256,256]{2,1,0:T(8,128)S(1)} %get-tuple-element.109), channel_id=1, source_target_pairs={{0,1},{1,0},{2,3},{3,2},{4,5},{5,4},{6,7},{7,6},{8,9},{9,8},{10,11... | collective-permute-start | bytes 1572872 | tf_op jit(solution)/shard_map/ppermute | solution.py:379
  203.9 38.4 %collective-permute-start.22 = (f32[2,768,256]{2,1,0:T(8,128)S(1)}, f32[2,768,256]{2,1,0:T(8,128)S(1)}, u32[]{:S(2)}, u32[]{:S(2)}) collective-permute-start(f32[2,768,256]{2,1,0:T(8,128)S(1)} %get-tuple-element.117), channel_id=1, source_target_pairs={{7,0},{0,1},{1,2},{2,3},{3,4},{4,5},{5,6},{6,7},{15,8},{8,9},{9,10... | collective-permute-start | bytes 4718600 | tf_op jit(solution)/shard_map/ppermute | solution.py:32
  205.3 37.1 %collective-permute-start.23 = (f32[3,256,256]{2,1,0:T(8,128)S(1)}, f32[3,256,256]{2,1,0:T(8,128)S(1)}, u32[]{:S(2)}, u32[]{:S(2)}) collective-permute-start(f32[3,256,256]{2,1,0:T(8,128)S(1)} %get-tuple-element.119), channel_id=1, source_target_pairs={{120,0},{0,8},{8,16},{16,24},{24,32},{32,40},{40,48},{48,56},{56,6... | collective-permute-start | bytes 2359304 | tf_op jit(solution)/shard_map/ppermute | solution.py:32
  243.0 22.2 %collective-permute-start.24 = (f32[1,2,256,256]{3,2,1,0:T(8,128)S(1)}, f32[1,2,256,256]{3,2,1,0:T(8,128)S(1)}, u32[]{:S(2)}, u32[]{:S(2)}) collective-permute-start(f32[1,2,256,256]{3,2,1,0:T(8,128)S(1)} %get-tuple-element.124), channel_id=1, source_target_pairs={{120,0},{0,8},{8,16},{16,24},{24,32},{32,40},{40,48},{48,56},{56,6... | collective-permute-start | bytes 1572872 | tf_op jit(solution)/shard_map/ppermute | solution.py:32

commit v2 on v1

--- a/solution.py
+++ b/solution.py
@@ -13,6 +13,7 @@
 TILE = 512
 WIDE = TILE + F
 HALF = F // 2
+PART = F // 4
 LANES = 128
 FRAMES_LIMIT = 22
 BESIDE = 6
@@ -173,7 +174,7 @@
     return lax.rem(lax.axis_index("col"), 2) == 0
 
 
-def hand_out(canvas, grads, zl_out, zr_out, up_out, mid_out, dn_out, g_out):
+def hand_out(canvas, grads, zl_out, zr_out, up_out, mid_out, dn_out, keep_out, send_out):
     zl_out[...] = canvas[:, :, :F]
     zr_out[...] = canvas[:, :, TILE:]
     up_out[:2] = canvas[:, :F, F:TILE]
@@ -181,27 +182,33 @@
     mid_out[...] = canvas[:, F:TILE, F:TILE]
     dn_out[:2] = canvas[:, TILE:, F:TILE]
     dn_out[2] = jnp.where(on_left_core(), canvas[0, TILE:, TILE:], canvas[0, TILE:, :F])
+    left_core = on_left_core()
     for p in range(3):
         for h in range(2):
             for t in range(2):
-                g_out[pl.ds(4 * p + 2 * t + h, HALF, stride=12), :] = grads[p, h * HALF : (h + 1) * HALF, t * LANES : (t + 1) * LANES]
+                a, b = (grads[p, (2 * k + h) * PART : (2 * k + h + 1) * PART, t * LANES : (t + 1) * LANES] for k in range(2))
+                at = pl.ds(4 * p + 2 * t + h, PART, stride=12)
+                keep_out[at, :] = jnp.where(left_core, a, b)
+                send_out[at, :] = jnp.where(left_core, b, a)
 
 
 def start_kernel(tile, probe, ob, pr, own):
     ob[:, :TILE, :TILE] = tile[...]
     pr[...] = probe[...]
-    me = lax.axis_index("row") * lax.axis_size("col") + lax.axis_index("col")
-    picked = lax.broadcasted_iota(jnp.int32, (HALF, LANES), 0) == me
+    col = lax.axis_index("col")
+    me = lax.axis_index("row") * (lax.axis_size("col") // 2) + col // 2
+    row = lax.broadcasted_iota(jnp.int32, (F, LANES), 0)
     rows = []
     for p in range(2):
         for t in range(2):
             for h in range(2):
-                rows.append(jnp.sum(jnp.where(picked, probe[p, h * HALF : (h + 1) * HALF, t * LANES : (t + 1) * LANES], 0.0), axis=0, keepdims=True))
+                picked = row == (2 * lax.rem(col, 2) + h) * PART + me
+                rows.append(jnp.sum(jnp.where(picked, probe[p, :, t * LANES : (t + 1) * LANES], 0.0), axis=0, keepdims=True))
     own[...] = jnp.concatenate(rows, 0)
 
 
 def first_kernel(mine, ia, ib, ic, amp, left, right, pr, tile, below, below_right, beside, corner, *rest):
-    ob, light, outs, (unused, canvas, grads, listed, glow) = rest[0], rest[1], rest[2:8], rest[8:]
+    ob, light, outs, (unused, canvas, grads, listed, glow) = rest[0], rest[1], rest[2:9], rest[9:]
     ob[:, TILE:, :F] = below[...]
     ob[:, TILE:, F:TILE] = below_right[...]
     ob[:, :TILE, TILE:] = beside[...]
@@ -211,11 +218,16 @@
     hand_out(canvas, grads, *outs)
 
 
-def gathered_probe(pg, pr):
+def gathered_probe(mine, other, pr):
+    left_core = on_left_core()
     for p in range(2):
         for h in range(2):
             for t in range(2):
-                pr[p, h * HALF : (h + 1) * HALF, t * LANES : (t + 1) * LANES] = pg[pl.ds(4 * p + 2 * t + h, HALF, stride=8), :]
+                at = pl.ds(4 * p + 2 * t + h, PART, stride=8)
+                a, b = mine[at, :], other[at, :]
+                for k in range(2):
+                    rows = slice((2 * k + h) * PART, (2 * k + h + 1) * PART)
+                    pr[p, rows, t * LANES : (t + 1) * LANES] = jnp.where(left_core == (k == 0), a, b)
 
 
 def refreshed(put, size, o, l, zl, zr, up, mid, dn, left_in, right_in, across):
@@ -237,9 +249,7 @@
                     put(p, rows, cols, o[p, rows, cols] + s * scale)
 
 
-def next_kernel(mine, ia, ib, ic, amp, left, right, pg, o, l, zl, zr, up, mid, dn, left_in, right_in, cup, cdn, sup, sdn, swap, *rest):
-    ob, light, outs, (pr, canvas, grads, listed, glow) = rest[0], rest[1], rest[2:8], rest[8:]
-
+def refresh_kernel(o, l, zl, zr, up, mid, dn, left_in, right_in, cup, cdn, sup, sdn, swap, ob):
     def put(p, rows, cols, value):
         ob[p, rows, cols] = value
 
@@ -254,13 +264,17 @@
         return jnp.where(left_core == (j == 2), inner, outer)
 
     refreshed(put, WIDE, o, l, zl, zr, up, mid, dn, left_in, right_in, across)
-    gathered_probe(pg, pr)
+
+
+def next_kernel(mine, ia, ib, ic, amp, left, right, pg, po, ob, *rest):
+    unused, light, outs, (pr, canvas, grads, listed, glow) = rest[0], rest[1], rest[2:9], rest[9:]
+    gathered_probe(pg, po, pr)
     visit_frames(mine, (ia, ib, ic), amp, left, right, ob, pr, canvas, glow, grads, listed)
     light[...] = glow[F : F + WIDE, F : F + WIDE]
     hand_out(canvas, grads, *outs)
 
 
-def last_kernel(pg, o, l, zl, up, mid, left_in, cdn, sdn, o_out, p_out):
+def last_kernel(o, l, zl, up, mid, left_in, cdn, sdn, o_out):
     def put(p, rows, cols, value):
         o_out[p, rows, cols] = value
 
@@ -268,7 +282,6 @@
         return cdn[p, here, :] if j == 1 else sdn[0, p, here, :]
 
     refreshed(put, TILE, o, l, zl, None, up, mid, None, left_in, None, across)
-    gathered_probe(pg, p_out)
 
 
 def middle_kernel(last, g, old, zl, left_in, *rest):
@@ -287,11 +300,11 @@
                     out[2] = jnp.where(left_core, b, a)
         swap[0] = cdn[2]
         swap[1] = cup[2]
-    s = jnp.sum(g[...].reshape(HALF // 2, 24, LANES), axis=0)
+    s = jnp.sum(g[...].reshape(PART // 2, 24, LANES), axis=0)
     s = s[:12] + s[12:]
     value = old[...] + s[:8] / (jnp.concatenate([s[8:], s[8:]], 0) + probe_damping)
     new[...] = value
-    spread[...] = jnp.broadcast_to(value[None], (HALF, 8, LANES)).reshape(HALF * 8, LANES)
+    spread[...] = jnp.broadcast_to(value[None], (PART, 8, LANES)).reshape(PART * 8, LANES)
 
 
 def f32(*shape):
@@ -321,13 +334,23 @@
     ]
     outs = (
         f32(2, WIDE, WIDE), f32(WIDE, WIDE), f32(2, WIDE, F), f32(2, WIDE, F),
-        f32(3, F, F), f32(2, F, F), f32(3, F, F), f32(HALF * 12, LANES),
+        f32(3, F, F), f32(2, F, F), f32(3, F, F), f32(PART * 12, LANES), f32(PART * 12, LANES),
     )
     return call(kernel, args, outs, scratch, limit=FRAMES_LIMIT, smem=(0, 1, 2, 3), alias=alias)
 
 
-def everyone(x):
-    return lax.all_to_all(x, ("row", "col"), 0, 0)
+def add_kernel(a, b, out):
+    out[...] = a[...] + b[...]
+
+
+def every_chip(x):
+    size = lax.axis_size("row") * lax.axis_size("col")
+    groups = [list(range(core, size, 2)) for core in range(2)]
+    return lax.all_to_all(x, ("row", "col"), 0, 0, axis_index_groups=groups)
+
+
+def other_core(x):
+    return lax.ppermute(x, "col", [(i, i ^ 1) for i in range(lax.axis_size("col"))])
 
 
 def shards(object_field, probe, amplitude, positions, counts):
@@ -349,18 +372,18 @@
     )
     for sweep in range(PASSES):
         last = sweep == PASSES - 1
-        ob, light, to_left, to_right, up, mid, down, grad = state
-        grad = grad.reshape(HALF, 3, 4, LANES)
+        ob, light, to_left, to_right, up, mid, down, keep, send = state
+        grad = call(add_kernel, (keep, other_core(send)), (f32(PART * 12, LANES),))[0].reshape(PART, 3, 4, LANES)
         from_left = passed_along(to_right, "col", 1)
         centre_down = passed_along(down, "row", 1)
         moved = [from_left, centre_down]
         if not last:
             moved += [passed_along(to_left, "col", -1), passed_along(up, "row", -1)]
         grad, to_left, to_right = lax.optimization_barrier((grad, to_left, to_right))
-        grad = everyone(grad)
+        grad = every_chip(grad)
         grad, moved = lax.optimization_barrier((grad, moved))
-        grad = grad.reshape(HALF * 12, LANES)
-        tail = (f32(8, LANES), f32(HALF * 8, LANES))
+        grad = grad.reshape(PART * 12, LANES)
+        tail = (f32(8, LANES), f32(PART * 8, LANES))
         if last:
             from_left, centre_down = moved
             side_down, own, spread = call(
@@ -376,19 +399,21 @@
                 (f32(3, F, F), f32(3, F, F), f32(2, F, F)) + tail,
             )
             sides = (side_up, side_down, swap)
-            swapped = lax.ppermute(swap, "col", [(i, i ^ 1) for i in range(lax.axis_size("col"))])
-            moved = (passed_along(side_up, "row", -1), passed_along(side_down, "row", 1), swapped)
+            moved = (passed_along(side_up, "row", -1), passed_along(side_down, "row", 1), other_core(swap))
         sides, spread = lax.optimization_barrier((sides, spread))
-        pg = everyone(spread.reshape(HALF, 2, 4, LANES)).reshape(HALF * 8, LANES)
+        pg = every_chip(spread.reshape(PART, 2, 4, LANES)).reshape(PART * 8, LANES)
+        po = other_core(pg)
         if last:
-            return call(
-                last_kernel, (pg, ob, light, to_left, up, mid, from_left, centre_down, moved[0]),
-                (f32(2, TILE, TILE), f32(2, F, F)),
-            )
-        state = call_frames(
-            next_kernel, mine, *infos, amp, left, right, pg, ob, light, to_left, to_right, up, mid, down,
-            from_left, from_right, centre_up, centre_down, *moved, alias={8: 0},
-        )
+            object_out = call(
+                last_kernel, (ob, light, to_left, up, mid, from_left, centre_down, moved[0]), (f32(2, TILE, TILE),),
+            )[0]
+            return object_out, call(gathered_probe, (pg, po), (f32(2, F, F),))[0]
+        ob = call(
+            refresh_kernel,
+            (ob, light, to_left, to_right, up, mid, down, from_left, from_right, centre_up, centre_down, *moved),
+            (f32(2, WIDE, WIDE),), alias={0: 0},
+        )[0]
+        state = call_frames(next_kernel, mine, *infos, amp, left, right, pg, po, ob, alias={9: 0})
 
 
 def solution(mesh):

time: 268 us -> 248 us (0.925); the launches traced: 267 us -> 250 us
  blocking collectives: 179 us -> 139 us
  starting transfers between devices: 42.6 us -> 57.4 us
  waiting for transfers between devices: 15.4 us -> 21.6 us
    all_to_all x6, blocking collectives: 179 us -> 139 us  [every_chip(): return lax.all_to_all(x, ('row', 'col'), 0, 0, axis_index_groups=groups)]
    ppermute x23, starting transfers between devices: 41.2 us -> 48.9 us  [passed_along(): return lax.ppermute(block, axis, route)]
    ppermute x2 -> x8, starting transfers between devices: 1.35 us -> 8.53 us  [other_core(): lax.ppermute(x, 'col', [(i, i ^ 1) for i in range(lax.axis_size('col'))])]
    ppermute x2 -> x8, waiting for transfers between devices: 0.01 us -> 6.33 us  [other_core(): lax.ppermute(x, 'col', [(i, i ^ 1) for i in range(lax.axis_size('col'))])]
    pallas_call x8 -> x14, Pallas kernels: 26.9 us -> 28.8 us  [call(): pl.pallas_call(kernel, out_shape=tuple(outs), in_specs=[SMEM if i in smem...]
  transfers between devices with their start and end apart: 25 -> 31, of which waited for: 3 -> 7; matrix products, arithmetic and copies ran while one was open for 0% -> 0% of each run, Pallas kernels for 0% -> 2%
where the time goes in v2:
time: 248 us; the launch traced here: 250 us
  blocking collectives  139 us (56%)
  starting transfers between devices  57.4 us (23%)
  Pallas kernels  28.8 us (12%)
  waiting for transfers between devices  21.6 us (9%)
    all_to_all x6, blocking collectives, every_chip(): return lax.all_to_all(x, ('row', 'col'), 0, 0, axis_index_groups=groups)  139 us
    ppermute x23, starting transfers between devices, passed_along(): return lax.ppermute(block, axis, route)  48.9 us
    pallas_call x14, Pallas kernels, call(): pl.pallas_call(kernel, out_shape=tuple(outs), in_specs=[SMEM if i in smem...  28.8 us
    ppermute x23, waiting for transfers between devices, passed_along(): return lax.ppermute(block, axis, route)  15.3 us
    ppermute x8, starting transfers between devices, other_core(): lax.ppermute(x, 'col', [(i, i ^ 1) for i in range(lax.axis_size('col'))])  8.53 us
    ppermute x8, waiting for transfers between devices, other_core(): lax.ppermute(x, 'col', [(i, i ^ 1) for i in range(lax.axis_size('col'))])  6.33 us
  transfers between devices with their start and end apart: 31, of which 7 were waited for; matrix products, arithmetic and copies ran while one was open for 0% of the time, Pallas kernels for 2%

profile of v2, /device:TPU:1, one launch (start us, length us, event | category | flops | bytes accessed | tf_op | source)
XLA Modules:
  0.0 250.2 jit_solution(16429240331753859681)
XLA Ops:
  0.6 1.4 fusion
  2.1 5.8 %collective-permute-start = (f32[2,256,256]{2,1,0:T(8,128)S(1)}, f32[2,256,256]{2,1,0:T(8,128)S(1)}, u32[]{:S(2)}, u32[]{:S(2)}) collective-permute-start(f32[2,256,256]{2,1,0:T(8,128)S(1)} %get-tuple-element.139), channel_id=1, source_target_pairs={{8,0},{16,8},{24,16},{32,24},{40,32},{48,40},{56,48},{64,56},{72,6... | collective-permute-start | bytes 1572872 | tf_op jit(solution)/shard_map/ppermute | solution.py:33
  7.9 0.1 slice.19
  8.1 1.0 collective-permute-start.6
  9.9 0.1 add_bitcast_fusion.mine
  10.0 3.0 %collective-permute-start.2 = (s32[1,16]{1,0:T(1,128)S(1)}, s32[1,16]{1,0:T(1,128)S(1)}, u32[]{:S(2)}, u32[]{:S(2)}) collective-permute-start(s32[1,16]{1,0:T(1,128)S(1)} %add_bitcast_fusion.mine), channel_id=1, source_target_pairs={{1,0},{2,1},{3,2},{4,3},{5,4},{6,5},{7,6},{0,7},{9,8},{10,9},{11,1... | collective-permute-start | bytes 200 | tf_op jit(solution)/shard_map/ppermute | solution.py:33
  13.0 0.5 collective-permute-start.5
  13.6 9.8 %collective-permute-done.2 = s32[1,16]{1,0:T(1,128)S(1)} collective-permute-done((s32[1,16]{1,0:T(1,128)S(1)}, s32[1,16]{1,0:T(1,128)S(1)}, u32[]{:S(2)}, u32[]{:S(2)}) %collective-permute-start.2) | collective-permute-done | bytes 96 | tf_op jit(solution)/shard_map/ppermute | solution.py:33
  23.4 1.3 collective-permute-start.7
  24.6 2.1 collective-permute-start.4
  26.8 0.3 shard_map.86
  27.0 2.7 %collective-permute-done.5.below_right = f32[2,256,256]{2,1,0:T(8,128)S(1)} collective-permute-done((f32[2,256,256]{2,1,0:T(8,128)S(1)}, f32[2,256,256]{2,1,0:T(8,128)S(1)}, u32[]{:S(2)}, u32[]{:S(2)}) %collective-permute-start.5) | collective-permute-done | bytes 524320 | tf_op jit(solution)/shard_map/ppermute | solution.py:33
  29.8 0.0 collective-permute-done.4.ic
  29.8 2.7 %collective-permute-done.3.ia = s32[3,16]{1,0:T(4,128)S(1)} collective-permute-done((s32[3,16]{1,0:T(4,128)S(1)}, s32[3,16]{1,0:T(4,128)S(1)}, u32[]{:S(2)}, u32[]{:S(2)}) %collective-permute-start.3) | collective-permute-done | bytes 224 | tf_op jit(solution)/shard_map/ppermute | solution.py:33
  32.5 7.0 %shard_map.87 = (f32[2,768,768]{2,1,0:T(8,128)S(1)}, f32[768,768]{1,0:T(8,128)S(1)}, f32[2,768,256]{2,1,0:T(8,128)S(1)}, f32[2,768,256]{2,1,0:T(8,128)S(1)}, f32...) custom-call(s32[1,16]{1,0:T(1,128)S(1)} %add_bitcast_fusion.mine, ...), custom_call_target="tpu_custom_call", output_to_operand_aliasing={{0}: (8, {})} | custom-call | tf_op jit(solution)/shard_map/pallas_call | solution.py:315
  39.5 4.0 %collective-permute-start.11 = (f32[2,768,256]{2,1,0:T(8,128)S(1)}, f32[2,768,256]{2,1,0:T(8,128)S(1)}, u32[]{:S(2)}, u32[]{:S(2)}) collective-permute-start(f32[2,768,256]{2,1,0:T(8,128)S(1)} %get-tuple-element.83.refs_2_.zl), channel_id=1, source_target_pairs={{1,0},{2,1},{3,2},{4,3},{5,4},{6,5},{7,6},{0,7},{9,8},{10,9},{11,1... | collective-permute-start | bytes 4718600 | tf_op jit(solution)/shard_map/ppermute | solution.py:33
  43.6 3.1 %collective-permute-start.9 = (f32[2,768,256]{2,1,0:T(8,128)S(1)}, f32[2,768,256]{2,1,0:T(8,128)S(1)}, u32[]{:S(2)}, u32[]{:S(2)}) collective-permute-start(f32[2,768,256]{2,1,0:T(8,128)S(1)} %get-tuple-element.85.refs_4_.zr), channel_id=1, source_target_pairs={{7,0},{0,1},{1,2},{2,3},{3,4},{4,5},{5,6},{6,7},{15,8},{8,9},{9,10... | collective-permute-start | bytes 4718600 | tf_op jit(solution)/shard_map/ppermute | solution.py:33
  46.7 4.8 %collective-permute-start.12 = (f32[3,256,256]{2,1,0:T(8,128)S(1)}, f32[3,256,256]{2,1,0:T(8,128)S(1)}, u32[]{:S(2)}, u32[]{:S(2)}) collective-permute-start(f32[3,256,256]{2,1,0:T(8,128)S(1)} %get-tuple-element.80.up), channel_id=1, source_target_pairs={{8,0},{16,8},{24,16},{32,24},{40,32},{48,40},{56,48},{64,56},{72,6... | collective-permute-start | bytes 2359304 | tf_op jit(solution)/shard_map/ppermute | solution.py:33
  51.5 1.7 collective-permute-done.8.b
  53.2 21.3 %all_to_all.30 = f32[64,3,4,128]{3,2,1,0:T(4,128)S(1)} all-to-all(f32[64,3,4,128]{3,2,1,0:T(4,128)S(1)} %bitcast.26), channel_id=1, replica_groups={{0,2,4,6,8,10,12,14,16,18,20,22,24,26,28,30,32,34,36,38,40,42,44,46,48,..., dimensions={0} | all-to-all | bytes 786432 | tf_op jit(solution)/shard_map/all_to_all | solution.py:349
  74.6 0.3 shard_map.89
  74.9 5.3 %collective-permute-start.14 = (f32[3,256,256]{2,1,0:T(8,128)S(1)}, f32[3,256,256]{2,1,0:T(8,128)S(1)}, u32[]{:S(2)}, u32[]{:S(2)}) collective-permute-start(f32[3,256,256]{2,1,0:T(8,128)S(1)} %get-tuple-element.89), channel_id=1, source_target_pairs={{8,0},{16,8},{24,16},{32,24},{40,32},{48,40},{56,48},{64,56},{72,6... | collective-permute-start | bytes 2359304 | tf_op jit(solution)/shard_map/ppermute | solution.py:33
  80.1 2.3 collective-permute-start.16
  82.4 23.3 %all_to_all.31 = f32[64,2,4,128]{3,2,1,0:T(4,128)S(1)} all-to-all(f32[64,2,4,128]{3,2,1,0:T(4,128)S(1)} %bitcast.36), channel_id=1, replica_groups={{0,2,4,6,8,10,12,14,16,18,20,22,24,26,28,30,32,34,36,38,40,42,44,46,48,..., dimensions={0} | all-to-all | bytes 524288 | tf_op jit(solution)/shard_map/all_to_all | solution.py:349
  105.7 2.3 collective-permute-start.13
  108.0 2.0 shard_map.90.ob
  110.0 6.9 %shard_map.91 = (f32[2,768,768]{2,1,0:T(8,128)S(1)}, f32[768,768]{1,0:T(8,128)S(1)}, f32[2,768,256]{2,1,0:T(8,128)S(1)}, f32[2,768,256]{2,1,0:T(8,128)S(1)}, f32...) custom-call(s32[1,16]{1,0:T(1,128)S(1)} %add_bitcast_fusion.mine, ...), custom_call_target="tpu_custom_call", output_to_operand_aliasing={{0}: (9, {})} | custom-call | tf_op jit(solution)/shard_map/pallas_call | solution.py:315
  116.8 0.8 collective-permute-start.20
  117.6 3.1 %collective-permute-start.18 = (f32[2,768,256]{2,1,0:T(8,128)S(1)}, f32[2,768,256]{2,1,0:T(8,128)S(1)}, u32[]{:S(2)}, u32[]{:S(2)}) collective-permute-start(f32[2,768,256]{2,1,0:T(8,128)S(1)} %get-tuple-element.108.refs_4_.zr), channel_id=1, source_target_pairs={{7,0},{0,1},{1,2},{2,3},{3,4},{4,5},{5,6},{6,7},{15,8},{8,9},{9,10... | collective-permute-start | bytes 4718600 | tf_op jit(solution)/shard_map/ppermute | solution.py:33
  120.7 4.8 %collective-permute-start.21 = (f32[3,256,256]{2,1,0:T(8,128)S(1)}, f32[3,256,256]{2,1,0:T(8,128)S(1)}, u32[]{:S(2)}, u32[]{:S(2)}) collective-permute-start(f32[3,256,256]{2,1,0:T(8,128)S(1)} %get-tuple-element.103.up), channel_id=1, source_target_pairs={{8,0},{16,8},{24,16},{32,24},{40,32},{48,40},{56,48},{64,56},{72,6... | collective-permute-start | bytes 2359304 | tf_op jit(solution)/shard_map/ppermute | solution.py:33
  125.5 1.7 collective-permute-done.17.b
  127.2 22.6 %all_to_all.32 = f32[64,3,4,128]{3,2,1,0:T(4,128)S(1)} all-to-all(f32[64,3,4,128]{3,2,1,0:T(4,128)S(1)} %bitcast.27), channel_id=1, replica_groups={{0,2,4,6,8,10,12,14,16,18,20,22,24,26,28,30,32,34,36,38,40,42,44,46,48,..., dimensions={0} | all-to-all | bytes 786432 | tf_op jit(solution)/shard_map/all_to_all | solution.py:349
  149.8 0.3 shard_map.93
  150.1 4.7 %collective-permute-start.23 = (f32[3,256,256]{2,1,0:T(8,128)S(1)}, f32[3,256,256]{2,1,0:T(8,128)S(1)}, u32[]{:S(2)}, u32[]{:S(2)}) collective-permute-start(f32[3,256,256]{2,1,0:T(8,128)S(1)} %get-tuple-element.112), channel_id=1, source_target_pairs={{8,0},{16,8},{24,16},{32,24},{40,32},{48,40},{56,48},{64,56},{72,6... | collective-permute-start | bytes 2359304 | tf_op jit(solution)/shard_map/ppermute | solution.py:33
  154.8 1.0 collective-permute-start.25
  155.8 24.6 %all_to_all.33 = f32[64,2,4,128]{3,2,1,0:T(4,128)S(1)} all-to-all(f32[64,2,4,128]{3,2,1,0:T(4,128)S(1)} %bitcast.37), channel_id=1, replica_groups={{0,2,4,6,8,10,12,14,16,18,20,22,24,26,28,30,32,34,36,38,40,42,44,46,48,..., dimensions={0} | all-to-all | bytes 524288 | tf_op jit(solution)/shard_map/all_to_all | solution.py:349
  180.4 1.7 collective-permute-start.22
  182.2 2.0 shard_map.94.ob
  184.1 6.8 %shard_map.95 = (f32[2,768,768]{2,1,0:T(8,128)S(1)}, f32[768,768]{1,0:T(8,128)S(1)}, f32[2,768,256]{2,1,0:T(8,128)S(1)}, f32[2,768,256]{2,1,0:T(8,128)S(1)}, f32...) custom-call(s32[1,16]{1,0:T(1,128)S(1)} %add_bitcast_fusion.mine, ...), custom_call_target="tpu_custom_call", output_to_operand_aliasing={{0}: (9, {})} | custom-call | tf_op jit(solution)/shard_map/pallas_call | solution.py:315
  191.0 4.6 %collective-permute-start.27 = (f32[2,768,256]{2,1,0:T(8,128)S(1)}, f32[2,768,256]{2,1,0:T(8,128)S(1)}, u32[]{:S(2)}, u32[]{:S(2)}) collective-permute-start(f32[2,768,256]{2,1,0:T(8,128)S(1)} %get-tuple-element.125), channel_id=1, source_target_pairs={{7,0},{0,1},{1,2},{2,3},{3,4},{4,5},{5,6},{6,7},{15,8},{8,9},{9,10... | collective-permute-start | bytes 4718600 | tf_op jit(solution)/shard_map/ppermute | solution.py:33
  195.6 1.7 collective-permute-done.26.b
  197.3 27.8 %all_to_all.34 = f32[64,3,4,128]{3,2,1,0:T(4,128)S(1)} all-to-all(f32[64,3,4,128]{3,2,1,0:T(4,128)S(1)} %bitcast.28), channel_id=1, replica_groups={{0,2,4,6,8,10,12,14,16,18,20,22,24,26,28,30,32,34,36,38,40,42,44,46,48,..., dimensions={0} | all-to-all | bytes 786432 | tf_op jit(solution)/shard_map/all_to_all | solution.py:349
  225.2 0.7 shard_map.97
  225.9 19.4 %all_to_all.35 = f32[64,2,4,128]{3,2,1,0:T(4,128)S(1)} all-to-all(f32[64,2,4,128]{3,2,1,0:T(4,128)S(1)} %bitcast.38), channel_id=1, replica_groups={{0,2,4,6,8,10,12,14,16,18,20,22,24,26,28,30,32,34,36,38,40,42,44,46,48,..., dimensions={0} | all-to-all | bytes 524288 | tf_op jit(solution)/shard_map/all_to_all | solution.py:349
  245.2 1.3 collective-permute-start.30
  246.5 1.2 collective-permute-done.30.other
  247.6 0.9 shard_map.99
  248.5 1.7 shard_map.98
  (52 shorter events, 0.3 us)
Async XLA Ops:
  0.6 7.3 %copy-start.3 = (f32[2,512,512]{2,1,0:T(8,128)S(1)}, f32[2,512,512]{2,1,0:T(8,128)}, u32[]{:S(2)}) copy-start(f32[2,512,512]{2,1,0:T(8,128)} %tile.1) | copy-start | bytes 6291460
  2.1 7.8 %copy-start.5 = (s32[1,1,4,2]{2,3,1,0:T(2,128)S(1)}, s32[1,1,4,2]{2,3,1,0:T(2,128)}, u32[]{:S(2)}) copy-start(s32[1,1,4,2]{2,3,1,0:T(2,128)} %param.10) | copy-start | bytes 100
  2.1 24.7 %copy-start.4 = (f32[2,256,256]{2,1,0:T(8,128)S(1)}, f32[2,256,256]{2,1,0:T(8,128)}, u32[]{:S(2)}) copy-start(f32[2,256,256]{2,1,0:T(8,128)} %probe.1) | copy-start | bytes 1572868
  2.1 21.3 %collective-permute-start = (f32[2,256,256]{2,1,0:T(8,128)S(1)}, f32[2,256,256]{2,1,0:T(8,128)S(1)}, u32[]{:S(2)}, u32[]{:S(2)}) collective-permute-start(f32[2,256,256]{2,1,0:T(8,128)S(1)} %get-tuple-element.139), channel_id=1, source_target_pairs={{8,0},{16,8},{24,16},{32,24},{40,32},{48,40},{56,48},{64,56},{72,6... | collective-permute-start | bytes 1572872 | tf_op jit(solution)/shard_map/ppermute | solution.py:33
  7.9 24.6 %copy-start.1 = (bf16[512,1536]{1,0:T(8,128)(2,1)S(1)}, bf16[512,1536]{1,0:T(8,128)(2,1)}, u32[]{:S(2)}) copy-start(bf16[512,1536]{1,0:T(8,128)(2,1)} %constant.6.clone.left) | copy-start | bytes 4718596
  8.1 24.5 %copy-start = (bf16[1536,512]{1,0:T(8,128)(2,1)S(1)}, bf16[1536,512]{1,0:T(8,128)(2,1)}, u32[]{:S(2)}) copy-start(bf16[1536,512]{1,0:T(8,128)(2,1)} %constant.7.clone.right) | copy-start | bytes 4718596
  8.1 24.5 %copy-start.2 = (f32[1,1,4,256,256]{4,3,2,1,0:T(8,128)S(1)}, f32[1,1,4,256,256]{4,3,2,1,0:T(8,128)}, u32[]{:S(2)}) copy-start(f32[1,1,4,256,256]{4,3,2,1,0:T(8,128)} %param.9) | copy-start | bytes 3145732
  8.1 24.4 %collective-permute-start.6 = (f32[2,512,256]{2,1,0:T(8,128)S(1)}, f32[2,512,256]{2,1,0:T(8,128)S(1)}, u32[]{:S(2)}, u32[]{:S(2)}) collective-permute-start(f32[2,512,256]{2,1,0:T(8,128)S(1)} %slice.19), channel_id=1, source_target_pairs={{1,0},{2,1},{3,2},{4,3},{5,4},{6,5},{7,6},{0,7},{9,8},{10,9},{11,1... | collective-permute-start | bytes 3145736 | tf_op jit(solution)/shard_map/ppermute | solution.py:33
  10.0 13.4 %collective-permute-start.2 = (s32[1,16]{1,0:T(1,128)S(1)}, s32[1,16]{1,0:T(1,128)S(1)}, u32[]{:S(2)}, u32[]{:S(2)}) collective-permute-start(s32[1,16]{1,0:T(1,128)S(1)} %add_bitcast_fusion.mine), channel_id=1, source_target_pairs={{1,0},{2,1},{3,2},{4,3},{5,4},{6,5},{7,6},{0,7},{9,8},{10,9},{11,1... | collective-permute-start | bytes 200 | tf_op jit(solution)/shard_map/ppermute | solution.py:33
  13.0 10.3 %collective-permute-start.1 = (s32[1,16]{1,0:T(1,128)S(1)}, s32[1,16]{1,0:T(1,128)S(1)}, u32[]{:S(2)}, u32[]{:S(2)}) collective-permute-start(s32[1,16]{1,0:T(1,128)S(1)} %add_bitcast_fusion.mine), channel_id=1, source_target_pairs={{7,0},{0,1},{1,2},{2,3},{3,4},{4,5},{5,6},{6,7},{15,8},{8,9},{9,10... | collective-permute-start | bytes 200 | tf_op jit(solution)/shard_map/ppermute | solution.py:33
  13.0 16.8 %collective-permute-start.5 = (f32[2,256,256]{2,1,0:T(8,128)S(1)}, f32[2,256,256]{2,1,0:T(8,128)S(1)}, u32[]{:S(2)}, u32[]{:S(2)}) collective-permute-start(f32[2,256,256]{2,1,0:T(8,128)S(1)} %get-tuple-element.138), channel_id=1, source_target_pairs={{8,0},{16,8},{24,16},{32,24},{40,32},{48,40},{56,48},{64,56},{72,6... | collective-permute-start | bytes 1572872 | tf_op jit(solution)/shard_map/ppermute | solution.py:33
  23.4 9.1 %collective-permute-start.7 = (f32[2,256,256]{2,1,0:T(8,128)S(1)}, f32[2,256,256]{2,1,0:T(8,128)S(1)}, u32[]{:S(2)}, u32[]{:S(2)}) collective-permute-start(f32[2,256,256]{2,1,0:T(8,128)S(1)} %collective-permute-done.below), channel_id=1, source_target_pairs={{1,0},{2,1},{3,2},{4,3},{5,4},{6,5},{7,6},{0,7},{9,8},{10,9},{11,1... | collective-permute-start | bytes 1572872 | tf_op jit(solution)/shard_map/ppermute | solution.py:33
  24.6 5.2 %collective-permute-start.4 = (s32[3,16]{1,0:T(4,128)S(1)}, s32[3,16]{1,0:T(4,128)S(1)}, u32[]{:S(2)}, u32[]{:S(2)}) collective-permute-start(s32[3,16]{1,0:T(4,128)S(1)} %pad_add_fusion.ib), channel_id=1, source_target_pairs={{8,0},{16,8},{24,16},{32,24},{40,32},{48,40},{56,48},{64,56},{72,6... | collective-permute-start | bytes 584 | tf_op jit(solution)/shard_map/ppermute | solution.py:33
  26.8 5.8 %collective-permute-start.3 = (s32[3,16]{1,0:T(4,128)S(1)}, s32[3,16]{1,0:T(4,128)S(1)}, u32[]{:S(2)}, u32[]{:S(2)}) collective-permute-start(s32[3,16]{1,0:T(4,128)S(1)} %pad_add_fusion.ib), channel_id=1, source_target_pairs={{120,0},{0,8},{8,16},{16,24},{24,32},{32,40},{40,48},{48,56},{56,6... | collective-permute-start | bytes 584 | tf_op jit(solution)/shard_map/ppermute | solution.py:33
  39.5 35.0 %collective-permute-start.11 = (f32[2,768,256]{2,1,0:T(8,128)S(1)}, f32[2,768,256]{2,1,0:T(8,128)S(1)}, u32[]{:S(2)}, u32[]{:S(2)}) collective-permute-start(f32[2,768,256]{2,1,0:T(8,128)S(1)} %get-tuple-element.83.refs_2_.zl), channel_id=1, source_target_pairs={{1,0},{2,1},{3,2},{4,3},{5,4},{6,5},{7,6},{0,7},{9,8},{10,9},{11,1... | collective-permute-start | bytes 4718600 | tf_op jit(solution)/shard_map/ppermute | solution.py:33
  43.6 31.0 %collective-permute-start.9 = (f32[2,768,256]{2,1,0:T(8,128)S(1)}, f32[2,768,256]{2,1,0:T(8,128)S(1)}, u32[]{:S(2)}, u32[]{:S(2)}) collective-permute-start(f32[2,768,256]{2,1,0:T(8,128)S(1)} %get-tuple-element.85.refs_4_.zr), channel_id=1, source_target_pairs={{7,0},{0,1},{1,2},{2,3},{3,4},{4,5},{5,6},{6,7},{15,8},{8,9},{9,10... | collective-permute-start | bytes 4718600 | tf_op jit(solution)/shard_map/ppermute | solution.py:33
  46.7 27.9 %collective-permute-start.10 = (f32[3,256,256]{2,1,0:T(8,128)S(1)}, f32[3,256,256]{2,1,0:T(8,128)S(1)}, u32[]{:S(2)}, u32[]{:S(2)}) collective-permute-start(f32[3,256,256]{2,1,0:T(8,128)S(1)} %get-tuple-element.79.dn), channel_id=1, source_target_pairs={{120,0},{0,8},{8,16},{16,24},{24,32},{32,40},{40,48},{48,56},{56,6... | collective-permute-start | bytes 2359304 | tf_op jit(solution)/shard_map/ppermute | solution.py:33
  46.7 27.9 %collective-permute-start.12 = (f32[3,256,256]{2,1,0:T(8,128)S(1)}, f32[3,256,256]{2,1,0:T(8,128)S(1)}, u32[]{:S(2)}, u32[]{:S(2)}) collective-permute-start(f32[3,256,256]{2,1,0:T(8,128)S(1)} %get-tuple-element.80.up), channel_id=1, source_target_pairs={{8,0},{16,8},{24,16},{32,24},{40,32},{48,40},{56,48},{64,56},{72,6... | collective-permute-start | bytes 2359304 | tf_op jit(solution)/shard_map/ppermute | solution.py:33
  51.4 1.7 collective-permute-start.8
  74.9 33.1 %collective-permute-start.14 = (f32[3,256,256]{2,1,0:T(8,128)S(1)}, f32[3,256,256]{2,1,0:T(8,128)S(1)}, u32[]{:S(2)}, u32[]{:S(2)}) collective-permute-start(f32[3,256,256]{2,1,0:T(8,128)S(1)} %get-tuple-element.89), channel_id=1, source_target_pairs={{8,0},{16,8},{24,16},{32,24},{40,32},{48,40},{56,48},{64,56},{72,6... | collective-permute-start | bytes 2359304 | tf_op jit(solution)/shard_map/ppermute | solution.py:33
  80.1 27.8 %collective-permute-start.15 = (f32[3,256,256]{2,1,0:T(8,128)S(1)}, f32[3,256,256]{2,1,0:T(8,128)S(1)}, u32[]{:S(2)}, u32[]{:S(2)}) collective-permute-start(f32[3,256,256]{2,1,0:T(8,128)S(1)} %get-tuple-element.90), channel_id=1, source_target_pairs={{120,0},{0,8},{8,16},{16,24},{24,32},{32,40},{40,48},{48,56},{56,6... | collective-permute-start | bytes 2359304 | tf_op jit(solution)/shard_map/ppermute | solution.py:33
  80.1 27.8 %collective-permute-start.16 = (f32[2,256,256]{2,1,0:T(8,128)S(1)}, f32[2,256,256]{2,1,0:T(8,128)S(1)}, u32[]{:S(2)}, u32[]{:S(2)}) collective-permute-start(f32[2,256,256]{2,1,0:T(8,128)S(1)} %get-tuple-element.91), channel_id=1, source_target_pairs={{0,1},{1,0},{2,3},{3,2},{4,5},{5,4},{6,7},{7,6},{8,9},{9,8},{10,11... | collective-permute-start | bytes 1572872 | tf_op jit(solution)/shard_map/ppermute | solution.py:353
  105.7 4.3 %collective-permute-start.13 = (f32[512,128]{1,0:T(8,128)S(1)}, f32[512,128]{1,0:T(8,128)S(1)}, u32[]{:S(2)}, u32[]{:S(2)}) collective-permute-start(f32[512,128]{1,0:T(8,128)S(1)} %bitcast.32), channel_id=1, source_target_pairs={{0,1},{1,0},{2,3},{3,2},{4,5},{5,4},{6,7},{7,6},{8,9},{9,8},{10,11... | collective-permute-start | bytes 786440 | tf_op jit(solution)/shard_map/ppermute | solution.py:353
  116.8 33.0 %collective-permute-start.20 = (f32[2,768,256]{2,1,0:T(8,128)S(1)}, f32[2,768,256]{2,1,0:T(8,128)S(1)}, u32[]{:S(2)}, u32[]{:S(2)}) collective-permute-start(f32[2,768,256]{2,1,0:T(8,128)S(1)} %get-tuple-element.106.refs_2_.zl), channel_id=1, source_target_pairs={{1,0},{2,1},{3,2},{4,3},{5,4},{6,5},{7,6},{0,7},{9,8},{10,9},{11,1... | collective-permute-start | bytes 4718600 | tf_op jit(solution)/shard_map/ppermute | solution.py:33
  117.6 32.2 %collective-permute-start.18 = (f32[2,768,256]{2,1,0:T(8,128)S(1)}, f32[2,768,256]{2,1,0:T(8,128)S(1)}, u32[]{:S(2)}, u32[]{:S(2)}) collective-permute-start(f32[2,768,256]{2,1,0:T(8,128)S(1)} %get-tuple-element.108.refs_4_.zr), channel_id=1, source_target_pairs={{7,0},{0,1},{1,2},{2,3},{3,4},{4,5},{5,6},{6,7},{15,8},{8,9},{9,10... | collective-permute-start | bytes 4718600 | tf_op jit(solution)/shard_map/ppermute | solution.py:33
  120.7 29.1 %collective-permute-start.19 = (f32[3,256,256]{2,1,0:T(8,128)S(1)}, f32[3,256,256]{2,1,0:T(8,128)S(1)}, u32[]{:S(2)}, u32[]{:S(2)}) collective-permute-start(f32[3,256,256]{2,1,0:T(8,128)S(1)} %get-tuple-element.102.dn), channel_id=1, source_target_pairs={{120,0},{0,8},{8,16},{16,24},{24,32},{32,40},{40,48},{48,56},{56,6... | collective-permute-start | bytes 2359304 | tf_op jit(solution)/shard_map/ppermute | solution.py:33
  120.7 29.1 %collective-permute-start.21 = (f32[3,256,256]{2,1,0:T(8,128)S(1)}, f32[3,256,256]{2,1,0:T(8,128)S(1)}, u32[]{:S(2)}, u32[]{:S(2)}) collective-permute-start(f32[3,256,256]{2,1,0:T(8,128)S(1)} %get-tuple-element.103.up), channel_id=1, source_target_pairs={{8,0},{16,8},{24,16},{32,24},{40,32},{48,40},{56,48},{64,56},{72,6... | collective-permute-start | bytes 2359304 | tf_op jit(solution)/shard_map/ppermute | solution.py:33
  125.5 1.7 collective-permute-start.17
  150.1 32.0 %collective-permute-start.23 = (f32[3,256,256]{2,1,0:T(8,128)S(1)}, f32[3,256,256]{2,1,0:T(8,128)S(1)}, u32[]{:S(2)}, u32[]{:S(2)}) collective-permute-start(f32[3,256,256]{2,1,0:T(8,128)S(1)} %get-tuple-element.112), channel_id=1, source_target_pairs={{8,0},{16,8},{24,16},{32,24},{40,32},{48,40},{56,48},{64,56},{72,6... | collective-permute-start | bytes 2359304 | tf_op jit(solution)/shard_map/ppermute | solution.py:33
  154.8 27.3 %collective-permute-start.24 = (f32[3,256,256]{2,1,0:T(8,128)S(1)}, f32[3,256,256]{2,1,0:T(8,128)S(1)}, u32[]{:S(2)}, u32[]{:S(2)}) collective-permute-start(f32[3,256,256]{2,1,0:T(8,128)S(1)} %get-tuple-element.113), channel_id=1, source_target_pairs={{120,0},{0,8},{8,16},{16,24},{24,32},{32,40},{40,48},{48,56},{56,6... | collective-permute-start | bytes 2359304 | tf_op jit(solution)/shard_map/ppermute | solution.py:33
  154.8 27.3 %collective-permute-start.25 = (f32[2,256,256]{2,1,0:T(8,128)S(1)}, f32[2,256,256]{2,1,0:T(8,128)S(1)}, u32[]{:S(2)}, u32[]{:S(2)}) collective-permute-start(f32[2,256,256]{2,1,0:T(8,128)S(1)} %get-tuple-element.114), channel_id=1, source_target_pairs={{0,1},{1,0},{2,3},{3,2},{4,5},{5,4},{6,7},{7,6},{8,9},{9,8},{10,11... | collective-permute-start | bytes 1572872 | tf_op jit(solution)/shard_map/ppermute | solution.py:353
  180.4 3.7 %collective-permute-start.22 = (f32[512,128]{1,0:T(8,128)S(1)}, f32[512,128]{1,0:T(8,128)S(1)}, u32[]{:S(2)}, u32[]{:S(2)}) collective-permute-start(f32[512,128]{1,0:T(8,128)S(1)} %bitcast.30), channel_id=1, source_target_pairs={{0,1},{1,0},{2,3},{3,2},{4,5},{5,4},{6,7},{7,6},{8,9},{9,8},{10,11... | collective-permute-start | bytes 786440 | tf_op jit(solution)/shard_map/ppermute | solution.py:353
  191.0 34.2 %collective-permute-start.27 = (f32[2,768,256]{2,1,0:T(8,128)S(1)}, f32[2,768,256]{2,1,0:T(8,128)S(1)}, u32[]{:S(2)}, u32[]{:S(2)}) collective-permute-start(f32[2,768,256]{2,1,0:T(8,128)S(1)} %get-tuple-element.125), channel_id=1, source_target_pairs={{7,0},{0,1},{1,2},{2,3},{3,4},{4,5},{5,6},{6,7},{15,8},{8,9},{9,10... | collective-permute-start | bytes 4718600 | tf_op jit(solution)/shard_map/ppermute | solution.py:33
  195.6 29.6 %collective-permute-start.28 = (f32[3,256,256]{2,1,0:T(8,128)S(1)}, f32[3,256,256]{2,1,0:T(8,128)S(1)}, u32[]{:S(2)}, u32[]{:S(2)}) collective-permute-start(f32[3,256,256]{2,1,0:T(8,128)S(1)} %get-tuple-element.130), channel_id=1, source_target_pairs={{120,0},{0,8},{8,16},{16,24},{24,32},{32,40},{40,48},{48,56},{56,6... | collective-permute-start | bytes 2359304 | tf_op jit(solution)/shard_map/ppermute | solution.py:33
  195.6 1.7 collective-permute-start.26
  225.9 22.7 %collective-permute-start.29 = (f32[1,2,256,256]{3,2,1,0:T(8,128)S(1)}, f32[1,2,256,256]{3,2,1,0:T(8,128)S(1)}, u32[]{:S(2)}, u32[]{:S(2)}) collective-permute-start(f32[1,2,256,256]{3,2,1,0:T(8,128)S(1)} %get-tuple-element.135), channel_id=1, source_target_pairs={{120,0},{0,8},{8,16},{16,24},{24,32},{32,40},{40,48},{48,56},{56,6... | collective-permute-start | bytes 1572872 | tf_op jit(solution)/shard_map/ppermute | solution.py:33
  245.2 2.4 collective-permute-start.30
